TPU v7x, 256 devices: a whole 4x4x8 slice. The times are simulated.
256 devices in a mesh: tile: 64 (over x, z, core), lev: 4 (over y).
Axes of the slice: x: 4, y: 4, z: 8, core: 2. Of those that a mesh axis runs over, the one named last changes fastest.
Arguments:
- cube_field: bfloat16 [128, 294912], P('lev', 'tile'), may hold values from -6 to 6
- margin: bfloat16 [9216, 64, 128], P('tile'), may hold values from -0.75 to 0.75
- pair_owner: int32 [9216], P('tile'), may hold values from 0 to 63, as said below
- pair_block: int32 [9216], P('tile'), may hold values from 0 to 143
- cube_area: float32 [294912], P('tile'), may hold values from 0.5 to 2
- band_area: float32 [768, 1536], P('tile'), may hold values from 0.5 to 2
- wave_order: int32 [768], replicated, may hold values from 0 to 767, each once
- legendre: bfloat16 [768, 2, 384, 384], P(('tile', 'lev')), may hold values from -0.3125 to 0.3125
- gauss_weight: float32 [384], replicated, may hold values from 0.3 to 1.5
- diffusion: float32 [128], replicated, may hold values from 0.3 to 30
Outputs:
- regridded: bfloat16 [128, 294912], P('lev', 'tile')
Inputs may be any that keep to these rules, and one draw needn't show every extreme that they name: `pair_owner`: among the pairs of one index of tile, one owner appears at most 6 times; one owner, drawn from the seed, appears exactly 6 times among the pairs of every index of tile. `wave_order`: each wavenumber 0 to 767 stands in exactly one slot.
All inputs are finite; a program needn't handle non-finite values.
Results may differ from a plain program's by a relative error of at most 0.013.
Values may be sent and summed in bfloat16 or wider, within the bound.
A program may use at most 128 MiB of HBM per device.

v0:
```python
import functools
import math

import jax
import jax.numpy as jnp
import numpy as np
from jax import lax
from jax.experimental import pallas as pl
from jax.experimental.pallas import tpu as pltpu
from jax.sharding import PartitionSpec as P

TRUNC = 766
MESH = pl.DeviceIdType.MESH
BF = jnp.bfloat16
F32 = jnp.float32
GROUP = 4
PAD_LAT = 16
VMEM_LIMIT = 56 * 2**20
NT = (((1,), (1,)), ((), ()))
TN = (((0,), (0,)), ((), ()))

XS, ZS, LEVS = 4, 8, 4
CHIPS = XS * ZS
TILES = 2 * CHIPS


def place():
    tile = lax.axis_index("tile")
    return tile, tile // (2 * ZS), (tile // 2) % ZS, tile % 2


def chip_at(x, z):
    return ((x + XS) % XS) * ZS + (z + ZS) % ZS


def greet():
    tile, _, _, _ = place()
    lev = lax.axis_index("lev")
    barrier = pltpu.get_barrier_semaphore()

    def one(step, carry):
        peer = (tile + step) % TILES
        pl.semaphore_signal(barrier, inc=1, device_id=(peer, lev), device_id_type=MESH)
        return carry

    lax.fori_loop(1, TILES, one, 0)
    for step in range(1, LEVS):
        peer = (tile, (lev + step) % LEVS)
        pl.semaphore_signal(barrier, inc=1, device_id=peer, device_id_type=MESH)
    pl.semaphore_wait(barrier, TILES - 1 + LEVS - 1)


def remote(src, dst, send, recv, peer, lev=None):
    return pltpu.make_async_remote_copy(
        src_ref=src,
        dst_ref=dst,
        send_sem=send,
        recv_sem=recv,
        device_id=(peer, lax.axis_index("lev") if lev is None else lev),
        device_id_type=MESH,
    )


def slot_of(tile):
    return (tile % 2) * CHIPS + tile // 2


def cos_sin(phase, turn):
    eighth = turn // 8
    octant = ((phase + eighth).astype(F32) * (4.0 / turn) + 0.5 / turn).astype(jnp.int32)
    angle = (phase - octant * (turn // 4)).astype(F32) * (2.0 * math.pi / turn)
    square = angle * angle
    cos = 1.0 + square * (
        -1 / 2 + square * (1 / 24 + square * (-1 / 720 + square * (1 / 40320)))
    )
    sin = angle * (
        1.0 + square * (-1 / 6 + square * (1 / 120 + square * (-1 / 5040 + square * (1 / 362880))))
    )
    odd = octant % 2 == 1
    base_c, base_s = jnp.where(odd, sin, cos), jnp.where(odd, cos, sin)
    flip_c = (octant == 1) | (octant == 2)
    flip_s = (octant == 2) | (octant == 3)
    return jnp.where(flip_c, -base_c, base_c), jnp.where(flip_s, -base_s, base_s)


def wrap(count, turn):
    return count - ((count.astype(F32) + 0.5) * (1.0 / turn)).astype(jnp.int32) * turn


def down_rows(row, width):
    first = lax.broadcasted_iota(jnp.int32, (16, row.shape[1]), 0) == 0
    spread = jnp.where(first, row.astype(F32), 0.0).astype(BF)
    return lax.dot_general(spread, jnp.ones((16, width), BF), TN, preferred_element_type=F32)


def to_spectra(
    chunks,
    codes,
    area_part,
    pick_rows,
    wave_rows,
    spectra,
    table_any,
    code_rows,
    arrived,
    code_in,
    totals,
    area,
    table,
    given,
    taken,
    folded,
    fourier,
    pair_send,
    pair_recv,
    swap_send,
    swap_recv,
    wave_send,
    wave_recv,
    code_send,
    code_recv,
    area_send,
    area_recv,
    local_sem,
):
    tile, x, z, core = place()
    lev = lax.axis_index("lev")
    chip = tile // 2
    partner = tile + 1 - 2 * core
    lats, lons = totals.shape
    half = lats // 2
    pairs, points = arrived.shape[1:]
    rows = GROUP * pairs
    per_row = lons // points
    greet()

    area[lev, core, chip] = area_part[...]

    def area_z(step):
        there = chip_at(x, z + step)
        here = area.at[lev, core, chip]
        sems = area_send.at[step], area_recv.at[step]
        return remote(here, here, *sems, 2 * there + core)

    def area_x(step):
        there = chip_at(x + step, z)
        here = area.at[lev, core, pl.ds(pl.multiple_of(x * ZS, ZS), ZS)]
        sems = area_send.at[ZS + step], area_recv.at[ZS + step]
        return remote(here, here, *sems, 2 * there + core)

    def area_y(step):
        here = area.at[lev, core]
        sems = area_send.at[ZS + XS + step], area_recv.at[ZS + XS + step]
        return remote(here, here, *sems, tile, (lev + step) % LEVS)

    def area_core(q):
        here = area.at[q, core]
        at = ZS + XS + LEVS + q
        return remote(here, here, area_send.at[at], area_recv.at[at], partner)

    for step in range(1, ZS):
        area_z(step).start()

    def code_copy(slot):
        there = chip_at(x + slot // ZS, z + slot % ZS)
        return remote(
            codes.at[slot % GROUP],
            code_in.at[slot],
            code_send.at[slot],
            code_recv.at[slot],
            2 * there + core,
        )

    def start_code(slot, carry):
        code_copy(slot).start()
        return carry

    lax.fori_loop(1, CHIPS, start_code, 0)
    code_in[0] = codes[0]

    def pair_copy(slot):
        there = chip_at(x + slot // ZS, z + slot % ZS)
        return remote(
            chunks.at[there],
            arrived.at[slot],
            pair_send.at[slot],
            pair_recv.at[slot],
            2 * there + core,
        )

    def start_pair(slot, carry):
        pair_copy(slot).start()
        return carry

    lax.fori_loop(1, CHIPS, start_pair, 0)
    arrived[0] = chunks[chip]

    strip = 64
    longitude = lax.broadcasted_iota(jnp.int32, (strip, points), 1)
    norm = 1.0 / math.sqrt(lons)

    def make_rows(step, carry):
        at = pl.ds(pl.multiple_of(step * strip, strip), strip)
        code = wave_rows[at, :]
        wave, part = code % 1024, code // 1024
        cos, sin = cos_sin(wrap(wave * longitude + part * (lons // 4), lons), lons)
        cos, sin = cos * norm, sin * norm
        turn_c, turn_s = cos_sin(wrap(wave * points, lons), lons)
        for block in range(per_row):
            table[at, block * points : (block + 1) * points] = cos.astype(BF)
            cos, sin = cos * turn_c - sin * turn_s, sin * turn_c + cos * turn_s
        return carry

    lax.fori_loop(0, table.shape[0] // strip, make_rows, 0)
    table_copy = pltpu.make_async_copy(table, table_any, local_sem.at[1])
    table_copy.start()

    for step in range(1, ZS):
        area_z(step).wait_recv()
    for step in range(1, XS):
        area_x(step).start()

    lat_index = lax.broadcasted_iota(jnp.int32, (lats, rows), 0)

    def add_group(group, first):
        for j in range(GROUP):
            if not (first and j == 0):
                code_copy(group * GROUP + j).wait_recv()
                pair_copy(group * GROUP + j).wait_recv()
        code = code_in[group * GROUP]
        for j in range(1, GROUP):
            code = code + code_in[group * GROUP + j]
        code_rows[group] = code
        code = code[:, :rows]
        one_hot = jnp.where(lat_index == code // 16, 1.0, 0.0).astype(BF)
        values = arrived[pl.ds(group * GROUP, GROUP)].reshape(rows, points)
        where = down_rows(code % 16, points).astype(BF)
        for b in range(0, per_row, 2):
            spread = jnp.concatenate(
                [jnp.where(where == float(b + i), values, jnp.zeros_like(values)) for i in range(2)],
                axis=1,
            )
            term = jnp.dot(one_hot, spread, preferred_element_type=F32)
            at = slice(b * points, (b + 2) * points)
            if first:
                totals[:, at] = term
            else:
                totals[:, at] += term

    def later_group(group, carry):
        add_group(group, False)
        return carry

    add_group(0, True)
    for step in range(1, XS):
        area_x(step).wait_recv()
    for step in range(1, LEVS):
        area_y(step).start()
    lax.fori_loop(1, 4, later_group, 0)
    for step in range(1, LEVS):
        area_y(step).wait_recv()
    for q in range(LEVS):
        area_core(q).start()
    lax.fori_loop(4, CHIPS // GROUP, later_group, 0)
    for q in range(LEVS):
        area_core(q).wait_recv()

    sign = (1 - 2 * core).astype(F32)
    quarters = LEVS
    width = lons // LEVS

    def weights(q, side):
        found = []
        for c in range(2):
            part = area[q, c, side * (CHIPS // 2) : (side + 1) * (CHIPS // 2)]
            part = part.reshape(-1, width)
            found.append(jnp.dot(pick_rows[side, c], part, preferred_element_type=F32))
        return found[0] + found[1]

    def swap_copy(q):
        return remote(
            given.at[q], taken.at[q], swap_send.at[q], swap_recv.at[q], partner
        )

    for q in range(quarters):
        at = slice(q * width, (q + 1) * width)
        north = totals[:half, at] * weights(q, 0)
        south = totals[half:, at] * weights(q, 1) * sign
        totals[:half, at] = north + south
        given[q] = (north - south).astype(BF)
        swap_copy(q).start()
    for q in range(quarters):
        at = slice(q * width, (q + 1) * width)
        swap_copy(q).wait_recv()
        folded[:, at] = (totals[:half, at] + taken[q].astype(F32)).astype(BF)

    share = fourier.shape[1]
    batch = ZS

    def wave_copy(peer):
        return remote(
            fourier.at[peer],
            spectra.at[slot_of(tile)],
            wave_send.at[peer],
            wave_recv.at[tile],
            peer,
        )

    def transform(step, carry):
        first = ((x + step // 2) % XS) * (2 * ZS) + ((z // (ZS // 2) + step) % 2) * batch
        at = pl.ds(pl.multiple_of(first * share, batch * share), batch * share)
        part = lax.dot_general(table[at, :], folded[...], NT, preferred_element_type=F32)
        fourier[pl.ds(first, batch)] = part.astype(BF).reshape(batch, share, half)
        for j in range(batch):
            peer = first + j

            @pl.when(peer != tile)
            def _():
                wave_copy(peer).start()

        return carry

    lax.fori_loop(0, TILES // batch, transform, 0)
    spectra[slot_of(tile)] = fourier[tile]

    def finish_wave(step, carry):
        peer = (tile + step) % TILES
        wave_copy(peer).wait_send()
        remote(
            fourier.at[peer],
            spectra.at[slot_of(peer)],
            wave_send.at[peer],
            wave_recv.at[peer],
            peer,
        ).wait_recv()
        return carry

    lax.fori_loop(1, TILES, finish_wave, 0)

    def finish_pair(slot, carry):
        pair_copy(slot).wait_send()
        return carry

    lax.fori_loop(1, CHIPS, finish_pair, 0)
    def finish_code(slot, carry):
        code_copy(slot).wait_send()
        return carry

    lax.fori_loop(1, CHIPS, finish_code, 0)
    for q in range(quarters):
        swap_copy(q).wait_send()
        area_core(q).wait_send()
    for step in range(1, ZS):
        area_z(step).wait_send()
    for step in range(1, XS):
        area_x(step).wait_send()
    for step in range(1, LEVS):
        area_y(step).wait_send()
    table_copy.wait()


def from_spectra(
    spectra,
    order,
    back_order,
    tables_any,
    response,
    table_any,
    code_rows,
    replies,
    tables,
    table,
    sorted_in,
    sorted_out,
    parts,
    returned,
    wide,
    given,
    taken,
    band,
    picked,
    wave_send,
    wave_recv,
    swap_send,
    swap_recv,
    pair_send,
    pair_recv,
    local_sem,
):
    tile, x, z, core = place()
    chip = tile // 2
    slots = tables.shape[0]
    half, lons = wide.shape
    pairs, points = picked.shape[1:]
    rows = GROUP * pairs
    per_row = lons // points
    share = parts.shape[1]
    mixed = 2 * CHIPS
    locals_in = [
        pltpu.make_async_copy(tables_any, tables, local_sem.at[0]),
        pltpu.make_async_copy(table_any, table, local_sem.at[1]),
    ]
    for copy in locals_in:
        copy.start()
    greet()

    for p in range(2):
        sorted_in[p] = jnp.dot(order[...], spectra[p], preferred_element_type=F32).astype(BF)
    locals_in[0].wait()

    def one_slot(slot, carry):
        at = pl.ds(pl.multiple_of(slot * mixed, mixed), mixed)
        for p in range(2):
            legendre = tables[slot, p]
            coefficient = lax.dot_general(
                sorted_in[p, at, :], legendre, NT, preferred_element_type=F32
            )
            scale = response[slot, p]
            spectrum = jnp.concatenate(
                [coefficient[:CHIPS] * scale, coefficient[CHIPS:] * scale], axis=0
            ).astype(BF)
            sorted_out[p, at, :] = jnp.dot(
                spectrum, legendre, preferred_element_type=F32
            ).astype(BF)
        return carry

    lax.fori_loop(0, slots, one_slot, 0)

    def wave_copy(peer):
        return remote(
            parts.at[peer], returned.at[tile], wave_send.at[peer], wave_recv.at[tile], peer
        )

    def send_back(step, carry):
        first = ((x + step) % XS) * ZS
        at = pl.ds(pl.multiple_of(first * share, ZS * share), ZS * share)
        for p in range(2):
            part = jnp.dot(back_order[at, :], sorted_out[p], preferred_element_type=F32)
            part = part.astype(BF).reshape(ZS, share, half)
            for j in range(ZS):
                peer = 2 * (first + j) + p
                parts[peer] = part[j]

                @pl.when(peer != tile)
                def _():
                    wave_copy(peer).start()

        return carry

    lax.fori_loop(0, XS, send_back, 0)
    returned[tile] = parts[tile]
    locals_in[1].wait()

    def wave_arrival(peer):
        return remote(
            parts.at[peer], returned.at[peer], wave_send.at[peer], wave_recv.at[peer], peer
        )

    def inverse(step):
        first = ((x + XS - step) % XS) * (2 * ZS)

        def wait_one(j, carry):
            @pl.when(first + j != tile)
            def _():
                wave_arrival(first + j).wait_recv()

            return carry

        lax.fori_loop(0, 2 * ZS, wait_one, 0)
        values = returned[pl.ds(first, 2 * ZS)].reshape(2 * ZS * share, half)
        at = pl.ds(pl.multiple_of(first * share, 2 * ZS * share), 2 * ZS * share)
        for c in range(0, lons, 512):
            term = lax.dot_general(
                values, table[at, c : c + 512], TN, preferred_element_type=F32
            )
            if step == 0:
                wide[:, c : c + 512] = term
            else:
                wide[:, c : c + 512] += term

    for step in range(XS):
        inverse(step)

    partner = tile + 1 - 2 * core
    sign = (1 - 2 * core).astype(F32)
    quarters = given.shape[0]
    width = given.shape[2]

    def swap_copy(q):
        return remote(
            given.at[q], taken.at[q], swap_send.at[q], swap_recv.at[q], partner
        )

    for q in range(quarters):
        given[q] = wide[:, q * width : (q + 1) * width].astype(BF)
        swap_copy(q).start()
    for q in range(quarters):
        at = slice(q * width, (q + 1) * width)
        swap_copy(q).wait_recv()
        mine, theirs = wide[:, at], taken[q].astype(F32)
        band[:half, at] = (mine + theirs).astype(BF)
        band[half:, at] = ((mine - theirs) * sign).astype(BF)

    def pair_copy(slot):
        there = chip_at(x - slot // ZS, z - slot % ZS)
        return remote(
            picked.at[slot],
            replies.at[chip],
            pair_send.at[slot],
            pair_recv.at[chip],
            2 * there + core,
        )

    lat_index = lax.broadcasted_iota(jnp.int32, (rows, points), 1).astype(F32)

    def answer(group, carry):
        code = code_rows[group][:, :rows]
        lat = code // 16
        lat = down_rows(lat // points, points) * points + down_rows(lat % points, points)
        one_hot = jnp.concatenate(
            [
                jnp.where(lat == lat_index + float(c), 1.0, 0.0).astype(BF)
                for c in range(0, 2 * half, points)
            ],
            axis=1,
        )
        where = down_rows(code % 16, points).astype(BF)
        chosen = jnp.zeros((rows, points), BF)
        for b in range(0, per_row, 2):
            found = jnp.dot(
                one_hot, band[:, b * points : (b + 2) * points], preferred_element_type=F32
            ).astype(BF)
            for i in range(2):
                chosen = jnp.where(
                    where == float(b + i), found[:, i * points : (i + 1) * points], chosen
                )
        picked[pl.ds(group * GROUP, GROUP)] = chosen.reshape(GROUP, pairs, points)
        for j in range(GROUP):
            slot = group * GROUP + j

            @pl.when(slot != 0)
            def _():
                pair_copy(slot).start()

        return carry

    lax.fori_loop(0, CHIPS // GROUP, answer, 0)
    replies[chip] = picked[0]

    def finish_pair(slot, carry):
        pair_copy(slot).wait_send()
        here = chip_at(x - slot // ZS, z - slot % ZS)
        remote(
            picked.at[slot],
            replies.at[here],
            pair_send.at[slot],
            pair_recv.at[here],
            2 * here + core,
        ).wait_recv()
        return carry

    lax.fori_loop(1, CHIPS, finish_pair, 0)

    def finish_wave(step, carry):
        wave_copy((tile + step) % TILES).wait_send()
        return carry

    lax.fori_loop(1, TILES, finish_wave, 0)
    for q in range(quarters):
        swap_copy(q).wait_send()


def slot_orders(slots):
    chip, part, slot = np.meshgrid(
        np.arange(CHIPS), np.arange(2), np.arange(slots), indexing="ij"
    )
    source = ((chip * 2 + part) * slots + slot).reshape(-1)
    target = ((slot * 2 + part) * CHIPS + chip).reshape(-1)
    order = np.zeros((source.size, source.size), np.float32)
    order[target, source] = 1.0
    return jnp.asarray(order, BF), jnp.asarray(order.T.copy(), BF)


def lat_picks(lat_dev, half):
    picks = np.zeros((2, 2, half, CHIPS // 2 * PAD_LAT), np.float32)
    for tile in range(TILES):
        for i in range(lat_dev):
            lat = tile * lat_dev + i
            side = int(lat >= half)
            to = lat if side == 0 else 2 * half - 1 - lat
            picks[side, tile % 2, to, (tile // 2) % (CHIPS // 2) * PAD_LAT + i] = 1.0
    return jnp.asarray(picks, BF)


def shards(
    cube_field,
    margin,
    pair_owner,
    pair_block,
    cube_area,
    band_area,
    wave_order,
    legendre,
    gauss_weight,
    diffusion,
):
    levs = lax.axis_size("lev")
    tile, x, z, core = place()
    lev = lax.axis_index("lev")
    fields, cell_count = cube_field.shape
    pairs, cells, points = margin.shape
    blocks = pairs // 2
    lat_dev, lons = band_area.shape
    per_row = lons // points
    lats = lat_dev * TILES
    half = lats // 2
    slots = wave_order.shape[0] // TILES
    own_slots = legendre.shape[0]
    share = 2 * slots
    width = lons // levs
    groups = CHIPS // GROUP

    lat = pair_owner * lat_dev + pair_block // per_row
    row = jnp.where(lat < half, lat, lats + half - 1 - lat)
    code = row * 16 + pair_block % per_row
    room = -(-GROUP * pairs // points) * points
    codes = jnp.stack(
        [jnp.pad(code, (j * pairs, room - (j + 1) * pairs))[None] for j in range(GROUP)]
    )

    own_lat = tile * lat_dev + jnp.arange(lat_dev, dtype=jnp.int32)
    own_weight = gauss_weight[jnp.where(own_lat < half, own_lat, lats - 1 - own_lat)]
    part = lax.dynamic_slice_in_dim(band_area, lev * width, width, axis=1)
    part = (own_weight[:, None] / part).astype(BF)
    area_part = jnp.pad(part, ((0, PAD_LAT - lat_dev), (0, 0)))
    tables = lax.all_gather(
        legendre.reshape(own_slots * 2 * half, half), "lev", axis=0, tiled=True
    ).reshape(slots, 2, half, half)

    margin_q = margin.reshape(blocks, 2, cells, points)
    chunks = jnp.einsum(
        "fbc,bkcg->fbkg",
        cube_field.reshape(fields, blocks, cells),
        margin_q,
        preferred_element_type=F32,
    )
    chunks = chunks.astype(BF).reshape(fields, pairs, points)

    parts = jnp.arange(2, dtype=jnp.int32)[None, :, None] * 1024
    wave_rows = (wave_order.reshape(TILES, 1, slots) + parts).reshape(-1, 1)
    wave_rows = jnp.broadcast_to(wave_rows, (TILES * share, points))

    waves = lax.dynamic_slice_in_dim(wave_order, tile * slots, slots)
    damping = lax.dynamic_slice_in_dim(diffusion, lev * fields, fields)
    degree = (
        waves[:, None, None]
        + 2 * jnp.arange(half, dtype=jnp.int32)[None, None, :]
        + jnp.arange(2, dtype=jnp.int32)[None, :, None]
    )
    growth = (degree * (degree + 1)).astype(F32) / float(TRUNC * (TRUNC + 1))
    doubled = jnp.where(waves == 0, 1.0, 2.0).astype(F32)[:, None, None, None]
    response = jnp.where(
        (degree <= TRUNC)[:, :, None, :],
        doubled / (1.0 + damping[None, None, :, None] * growth[:, :, None, :]),
        0.0,
    )

    vmem = pl.BlockSpec(memory_space=pltpu.VMEM)
    anywhere = pl.BlockSpec(memory_space=pl.ANY)
    dma = pltpu.SemaphoreType.DMA
    spectra, table, code_rows = pl.pallas_call(
        to_spectra,
        out_shape=(
            jax.ShapeDtypeStruct((TILES, share, half), BF),
            jax.ShapeDtypeStruct((TILES * share, lons), BF),
            jax.ShapeDtypeStruct((groups, 1, room), jnp.int32),
        ),
        in_specs=[vmem] * 5,
        out_specs=(vmem, anywhere, vmem),
        scratch_shapes=[
            pltpu.VMEM((CHIPS, pairs, points), BF),
            pltpu.VMEM((CHIPS, 1, room), jnp.int32),
            pltpu.VMEM((lats, lons), F32),
            pltpu.VMEM((levs, 2, CHIPS, PAD_LAT, width), BF),
            pltpu.VMEM((TILES * share, lons), BF),
            pltpu.VMEM((levs, half, width), BF),
            pltpu.VMEM((levs, half, width), BF),
            pltpu.VMEM((half, lons), BF),
            pltpu.VMEM((TILES, share, half), BF),
            dma((CHIPS,)),
            dma((CHIPS,)),
            dma((levs,)),
            dma((levs,)),
            dma((TILES,)),
            dma((TILES,)),
            dma((CHIPS,)),
            dma((CHIPS,)),
            dma((ZS + XS + 2 * LEVS,)),
            dma((ZS + XS + 2 * LEVS,)),
            dma((2,)),
        ],
        compiler_params=pltpu.CompilerParams(
            collective_id=0, has_side_effects=True, vmem_limit_bytes=VMEM_LIMIT
        ),
    )(chunks, codes, area_part, lat_picks(lat_dev, half), wave_rows)

    order, back_order = slot_orders(slots)
    mixed = CHIPS * share
    replies = pl.pallas_call(
        from_spectra,
        out_shape=jax.ShapeDtypeStruct((CHIPS, pairs, points), BF),
        in_specs=[vmem, vmem, vmem, anywhere, vmem, anywhere, vmem],
        out_specs=vmem,
        scratch_shapes=[
            pltpu.VMEM((slots, 2, half, half), BF),
            pltpu.VMEM((TILES * share, lons), BF),
            pltpu.VMEM((2, mixed, half), BF),
            pltpu.VMEM((2, mixed, half), BF),
            pltpu.VMEM((TILES, share, half), BF),
            pltpu.VMEM((TILES, share, half), BF),
            pltpu.VMEM((half, lons), F32),
            pltpu.VMEM((levs, half, width), BF),
            pltpu.VMEM((levs, half, width), BF),
            pltpu.VMEM((lats, lons), BF),
            pltpu.VMEM((CHIPS, pairs, points), BF),
            dma((TILES,)),
            dma((TILES,)),
            dma((levs,)),
            dma((levs,)),
            dma((CHIPS,)),
            dma((CHIPS,)),
            dma((2,)),
        ],
        compiler_params=pltpu.CompilerParams(
            collective_id=1, has_side_effects=True, vmem_limit_bytes=VMEM_LIMIT
        ),
    )(
        spectra.reshape(2, mixed, half),
        order,
        back_order,
        tables,
        response,
        table,
        code_rows,
    )

    cube = jnp.einsum(
        "fbkg,bkcg->fbc",
        replies.reshape(fields, blocks, 2, points),
        margin_q,
        preferred_element_type=F32,
    )
    cube = cube / cube_area.reshape(blocks, cells)[None]
    return cube.astype(BF).reshape(fields, cell_count)


def solution(mesh):
    in_specs = (
        P("lev", "tile"),
        P("tile", None, None),
        P("tile"),
        P("tile"),
        P("tile"),
        P("tile", None),
        P(),
        P(("tile", "lev"), None, None, None),
        P(),
        P(),
    )
    out_specs = P("lev", "tile")
    return jax.shard_map(shards, mesh=mesh, in_specs=in_specs, out_specs=out_specs, check_vma=False)
```

profile of v0, /device:TPU:1, one launch (start us, length us, event | category | flops | bytes accessed | tf_op | source)
XLA Modules:
  0.0 225.1 jit_solution(18062812320565171117)
XLA Ops:
  6.5 0.0 all-gather.2.cloned.1.call-start
  6.6 0.7 all-gather.2.cloned.1.call-update
  7.3 0.1 copy-done.6
  7.4 0.0 copy-done.5
  7.4 0.1 fusion.14
  7.5 0.2 copy-done.2
  7.7 0.3 reshape.119
  8.0 0.3 copy-done
  8.3 0.5 fusion
  8.8 0.0 copy-start.4
  8.8 0.0 copy-start.3
  8.8 0.0 copy-start.7
  8.8 0.0 copy-start.1
  8.8 1.9 copy.18
  10.8 0.1 add.138
  10.9 0.1 broadcast_add_fusion
  11.0 0.1 add.142
  11.1 0.1 div.46
  11.2 0.1 dynamic_slice.11
  11.3 0.7 gather_fusion
  11.9 0.8 divide_convert_fusion.1
  12.8 0.6 pad.24.area_part
  13.4 0.6 pad_add_fusion.codes
  14.0 1.2 broadcast_in_dim.18.wave_rows
  15.1 110.8 %shard_map.127 = (bf16[64,24,384]{2,1,0:T(8,128)(2,1)}, bf16[1536,1536]{1,0:T(8,128)(2,1)}, s32[8,1,640]{2,1,0:T(1,128)}) custom-call(bf16[32,144,128]{2,1,0:T(8,128)(2,1)} %bitcast.25, s32[4,1,640]{2,1,0:T(1,128)} %pad_add_fusion.codes, bf16[16,384]{1,0:T(8,128)(2,1)} %pad.24.area_part, bf16[2,2,384,256]{3,2,1,0:T(8,128)(2,1)} %constant.75.clone.pick_rows, ...), custom_call_target="tpu_custom_call" | custom-call | tf_op jit(solution)/shard_map/pallas_call | solution.py:671
  125.9 0.1 compare_select_fusion.3
  126.0 0.1 broadcast_add_fusion.1
  126.1 1.3 divide_select_fusion.response
  127.4 87.5 %shard_map.128 = bf16[32,144,128]{2,1,0:T(8,128)(2,1)} custom-call(bf16[2,768,384]{2,1,0:T(8,128)(2,1)} %bitcast.28, bf16[768,768]{1,0:T(8,128)(2,1)} %constant.76.clone.order, bf16[768,768]{1,0:T(8,128)(2,1)} %constant.77.clone.back_order, bf16[12,2,384,384]{3,2,1,0:T(8,128)(2,1)} %bitcast.24, f32[12,2,32,384]{3,2,1,0:T(8,128)} %divide_select_fusion.response, ...), custom_call_target="tpu_custom_call" | custom-call | tf_op jit(solution)/shard_map/pallas_call | solution.py:709
  215.0 2.0 fusion.4
  217.0 0.2 copy.20
  217.2 1.1 reshape.125
  (20 shorter events, 0.1 us)
Async XLA Ops:
  6.5 1.8 copy-start
  6.5 0.8 copy-start.6
  6.5 0.8 copy-start.5
  6.5 1.1 copy-start.2
  6.5 120.9 %all-gather.2.cloned.1.call-start = ((), (), s32[]{:S(2)}) async-start(), calls=%async_computation | async-start | bytes 8847360 | tf_op jit(solution)/shard_map/all_gather | solution.py:636
  8.8 2.0 copy-start.4
  8.8 2.3 %copy-start.3 = (f32[4608]{0:T(1024)S(1)}, f32[4608]{0:T(1024)}, u32[]{:S(2)}) copy-start(f32[4608]{0:T(1024)} %param.17) | copy-start | bytes 55300
  8.8 2.4 %copy-start.7 = (f32[128]{0:T(128)S(1)}, f32[128]{0:T(128)}, u32[]{:S(2)}) copy-start(f32[128]{0:T(128)} %param.22) | copy-start | bytes 1540
  8.8 2.5 %copy-start.1 = (f32[384]{0:T(512)S(1)}, f32[384]{0:T(512)}, u32[]{:S(2)}) copy-start(f32[384]{0:T(512)} %param.21) | copy-start | bytes 4612
Sparse Core Ops, SparseCore 0:
  9.2 95.4 all-gather.1
where the time goes:
time: 225 us
  Pallas kernels  198 us (88%)
  between operations  13.6 us (6%)
  local copies, waits for them, and re-layouts  7.07 us (3%)
  other arithmetic  3.06 us (1%)
  matrix products  2.47 us (1%)
    pallas_call x1, Pallas kernels, shards(): pl.pallas_call(to_spectra, out_shape=(jax.ShapeDtypeStruct((TILES, share,...  111 us
    pallas_call x1, Pallas kernels, shards(): pl.pallas_call(from_spectra, out_shape=jax.ShapeDtypeStruct((CHIPS, pairs...  87.5 us
  transfers between devices with their start and end apart: 1, of which 0 were waited for; matrix products, arithmetic and copies ran while one was open for 4% of the time, Pallas kernels for 49%

commit v1 on v0

--- a/solution.py
+++ b/solution.py
@@ -93,34 +93,58 @@
     return lax.dot_general(spread, jnp.ones((16, width), BF), TN, preferred_element_type=F32)
 
 
-def to_spectra(
+def regrid(
     chunks,
     codes,
     area_part,
     pick_rows,
-    wave_rows,
-    spectra,
-    table_any,
-    code_rows,
+    wave_codes,
+    wave_order,
+    damping,
+    legendre,
+    order,
+    back_order,
+    replies,
     arrived,
     code_in,
+    code_rows,
     totals,
     area,
     table,
+    tables,
+    response,
     given,
     taken,
     folded,
     fourier,
-    pair_send,
-    pair_recv,
-    swap_send,
-    swap_recv,
-    wave_send,
-    wave_recv,
+    spectra,
+    sorted_in,
+    sorted_out,
+    parts,
+    returned,
+    wide,
+    sent_back,
+    got_back,
+    band,
+    picked,
+    chunk_send,
+    chunk_recv,
     code_send,
     code_recv,
     area_send,
     area_recv,
+    table_send,
+    table_recv,
+    swap_send,
+    swap_recv,
+    fourier_send,
+    fourier_recv,
+    wave_send,
+    wave_recv,
+    return_send,
+    return_recv,
+    pair_send,
+    pair_recv,
     local_sem,
 ):
     tile, x, z, core = place()
@@ -161,6 +185,41 @@
     for step in range(1, ZS):
         area_z(step).start()
 
+    own = legendre.shape[0]
+
+    def own_tables(first, count):
+        return tables.at[pl.ds(own * lev + first, count)]
+
+    keep_tables = pltpu.make_async_copy(legendre, own_tables(0, own), local_sem.at[0])
+    keep_tables.start()
+
+    def give_tables(piece, way):
+        first, count = ((0, own // 3), (own // 3, own - own // 3))[piece]
+        at = 2 * piece + way
+        return remote(
+            legendre.at[pl.ds(first, count)],
+            own_tables(first, count),
+            table_send.at[at],
+            table_recv.at[at],
+            tile,
+            (lev + (1, LEVS - 1)[way]) % LEVS,
+        )
+
+    def pass_tables(way):
+        from_lev = (lev + (LEVS - 1, 1)[way]) % LEVS
+        here = tables.at[pl.ds(own * from_lev + way * (own // 2), own // 2)]
+        return remote(
+            here,
+            here,
+            table_send.at[4 + way],
+            table_recv.at[4 + way],
+            tile,
+            (lev + (1, LEVS - 1)[way]) % LEVS,
+        )
+
+    for way in range(2):
+        give_tables(0, way).start()
+
     def code_copy(slot):
         there = chip_at(x + slot // ZS, z + slot % ZS)
         return remote(
@@ -178,30 +237,32 @@
     lax.fori_loop(1, CHIPS, start_code, 0)
     code_in[0] = codes[0]
 
-    def pair_copy(slot):
+    def chunk_copy(slot):
         there = chip_at(x + slot // ZS, z + slot % ZS)
         return remote(
             chunks.at[there],
             arrived.at[slot],
-            pair_send.at[slot],
-            pair_recv.at[slot],
+            chunk_send.at[slot],
+            chunk_recv.at[slot],
             2 * there + core,
         )
 
-    def start_pair(slot, carry):
-        pair_copy(slot).start()
-        return carry
-
-    lax.fori_loop(1, CHIPS, start_pair, 0)
+    def start_chunk(slot, carry):
+        chunk_copy(slot).start()
+        return carry
+
+    lax.fori_loop(1, CHIPS, start_chunk, 0)
     arrived[0] = chunks[chip]
 
-    strip = 64
+    strip = points
     longitude = lax.broadcasted_iota(jnp.int32, (strip, points), 1)
     norm = 1.0 / math.sqrt(lons)
 
     def make_rows(step, carry):
         at = pl.ds(pl.multiple_of(step * strip, strip), strip)
-        code = wave_rows[at, :]
+        code = wave_codes[:, at]
+        code = down_rows(code // 64, points) * 64.0 + down_rows(code % 64, points)
+        code = code.astype(jnp.int32)
         wave, part = code % 1024, code // 1024
         cos, sin = cos_sin(wrap(wave * longitude + part * (lons // 4), lons), lons)
         cos, sin = cos * norm, sin * norm
@@ -212,21 +273,33 @@
         return carry
 
     lax.fori_loop(0, table.shape[0] // strip, make_rows, 0)
-    table_copy = pltpu.make_async_copy(table, table_any, local_sem.at[1])
-    table_copy.start()
 
     for step in range(1, ZS):
         area_z(step).wait_recv()
     for step in range(1, XS):
         area_x(step).start()
 
+    slots = response.shape[0]
+
+    def make_response(slot, carry):
+        wave = wave_order[tile * slots + slot]
+        doubled = jnp.where(wave == 0, 1.0, 2.0).astype(F32)
+        for p in range(2):
+            degree = wave + p + 2 * lax.broadcasted_iota(jnp.int32, (1, half), 1)
+            growth = (degree * (degree + 1)).astype(F32) * (1.0 / (TRUNC * (TRUNC + 1)))
+            value = doubled / (1.0 + damping[...] * growth)
+            response[slot, p] = jnp.where(degree <= TRUNC, value, 0.0)
+        return carry
+
+    lax.fori_loop(0, slots, make_response, 0)
+
     lat_index = lax.broadcasted_iota(jnp.int32, (lats, rows), 0)
 
     def add_group(group, first):
         for j in range(GROUP):
             if not (first and j == 0):
                 code_copy(group * GROUP + j).wait_recv()
-                pair_copy(group * GROUP + j).wait_recv()
+                chunk_copy(group * GROUP + j).wait_recv()
         code = code_in[group * GROUP]
         for j in range(1, GROUP):
             code = code + code_in[group * GROUP + j]
@@ -256,6 +329,8 @@
         area_x(step).wait_recv()
     for step in range(1, LEVS):
         area_y(step).start()
+    for way in range(2):
+        give_tables(1, way).start()
     lax.fori_loop(1, 4, later_group, 0)
     for step in range(1, LEVS):
         area_y(step).wait_recv()
@@ -297,12 +372,12 @@
     share = fourier.shape[1]
     batch = ZS
 
-    def wave_copy(peer):
+    def fourier_copy(peer):
         return remote(
             fourier.at[peer],
             spectra.at[slot_of(tile)],
-            wave_send.at[peer],
-            wave_recv.at[tile],
+            fourier_send.at[peer],
+            fourier_recv.at[tile],
             peer,
         )
 
@@ -316,126 +391,65 @@
 
             @pl.when(peer != tile)
             def _():
-                wave_copy(peer).start()
+                fourier_copy(peer).start()
 
         return carry
 
     lax.fori_loop(0, TILES // batch, transform, 0)
     spectra[slot_of(tile)] = fourier[tile]
-
-    def finish_wave(step, carry):
+    for way in range(2):
+        for piece in range(2):
+            give_tables(piece, way).wait_recv()
+        pass_tables(way).start()
+
+    def finish_fourier(step, carry):
         peer = (tile + step) % TILES
-        wave_copy(peer).wait_send()
+        fourier_copy(peer).wait_send()
         remote(
             fourier.at[peer],
             spectra.at[slot_of(peer)],
-            wave_send.at[peer],
-            wave_recv.at[peer],
+            fourier_send.at[peer],
+            fourier_recv.at[peer],
             peer,
         ).wait_recv()
         return carry
 
-    lax.fori_loop(1, TILES, finish_wave, 0)
-
-    def finish_pair(slot, carry):
-        pair_copy(slot).wait_send()
-        return carry
-
-    lax.fori_loop(1, CHIPS, finish_pair, 0)
-    def finish_code(slot, carry):
-        code_copy(slot).wait_send()
-        return carry
-
-    lax.fori_loop(1, CHIPS, finish_code, 0)
-    for q in range(quarters):
-        swap_copy(q).wait_send()
-        area_core(q).wait_send()
-    for step in range(1, ZS):
-        area_z(step).wait_send()
-    for step in range(1, XS):
-        area_x(step).wait_send()
-    for step in range(1, LEVS):
-        area_y(step).wait_send()
-    table_copy.wait()
-
-
-def from_spectra(
-    spectra,
-    order,
-    back_order,
-    tables_any,
-    response,
-    table_any,
-    code_rows,
-    replies,
-    tables,
-    table,
-    sorted_in,
-    sorted_out,
-    parts,
-    returned,
-    wide,
-    given,
-    taken,
-    band,
-    picked,
-    wave_send,
-    wave_recv,
-    swap_send,
-    swap_recv,
-    pair_send,
-    pair_recv,
-    local_sem,
-):
-    tile, x, z, core = place()
-    chip = tile // 2
-    slots = tables.shape[0]
-    half, lons = wide.shape
-    pairs, points = picked.shape[1:]
-    rows = GROUP * pairs
-    per_row = lons // points
-    share = parts.shape[1]
+    lax.fori_loop(1, TILES, finish_fourier, 0)
+
+    def wave_copy(peer):
+        return remote(
+            parts.at[peer], returned.at[tile], wave_send.at[peer], wave_recv.at[tile], peer
+        )
+
     mixed = 2 * CHIPS
-    locals_in = [
-        pltpu.make_async_copy(tables_any, tables, local_sem.at[0]),
-        pltpu.make_async_copy(table_any, table, local_sem.at[1]),
-    ]
-    for copy in locals_in:
-        copy.start()
-    greet()
-
+    for way in range(2):
+        pass_tables(way).wait_recv()
+    keep_tables.wait()
     for p in range(2):
-        sorted_in[p] = jnp.dot(order[...], spectra[p], preferred_element_type=F32).astype(BF)
-    locals_in[0].wait()
-
-    def one_slot(slot, carry):
-        at = pl.ds(pl.multiple_of(slot * mixed, mixed), mixed)
-        for p in range(2):
-            legendre = tables[slot, p]
+        rows_in = spectra[p * CHIPS : (p + 1) * CHIPS].reshape(CHIPS * share, half)
+        sorted_in[...] = jnp.dot(order[...], rows_in, preferred_element_type=F32).astype(BF)
+
+        def one_slot(slot, carry):
+            at = pl.ds(pl.multiple_of(slot * mixed, mixed), mixed)
+            legendre_at = tables[2 * slot + p]
             coefficient = lax.dot_general(
-                sorted_in[p, at, :], legendre, NT, preferred_element_type=F32
+                sorted_in[at, :], legendre_at, NT, preferred_element_type=F32
             )
             scale = response[slot, p]
             spectrum = jnp.concatenate(
                 [coefficient[:CHIPS] * scale, coefficient[CHIPS:] * scale], axis=0
             ).astype(BF)
-            sorted_out[p, at, :] = jnp.dot(
-                spectrum, legendre, preferred_element_type=F32
+            sorted_out[at, :] = jnp.dot(
+                spectrum, legendre_at, preferred_element_type=F32
             ).astype(BF)
-        return carry
-
-    lax.fori_loop(0, slots, one_slot, 0)
-
-    def wave_copy(peer):
-        return remote(
-            parts.at[peer], returned.at[tile], wave_send.at[peer], wave_recv.at[tile], peer
-        )
-
-    def send_back(step, carry):
-        first = ((x + step) % XS) * ZS
-        at = pl.ds(pl.multiple_of(first * share, ZS * share), ZS * share)
-        for p in range(2):
-            part = jnp.dot(back_order[at, :], sorted_out[p], preferred_element_type=F32)
+            return carry
+
+        lax.fori_loop(0, slots, one_slot, 0)
+
+        def send_back(step, carry):
+            first = ((x + step) % XS) * ZS
+            at = pl.ds(pl.multiple_of(first * share, ZS * share), ZS * share)
+            part = jnp.dot(back_order[at, :], sorted_out[...], preferred_element_type=F32)
             part = part.astype(BF).reshape(ZS, share, half)
             for j in range(ZS):
                 peer = 2 * (first + j) + p
@@ -445,11 +459,10 @@
                 def _():
                     wave_copy(peer).start()
 
-        return carry
-
-    lax.fori_loop(0, XS, send_back, 0)
+            return carry
+
+        lax.fori_loop(0, XS, send_back, 0)
     returned[tile] = parts[tile]
-    locals_in[1].wait()
 
     def wave_arrival(peer):
         return remote(
@@ -481,23 +494,18 @@
     for step in range(XS):
         inverse(step)
 
-    partner = tile + 1 - 2 * core
-    sign = (1 - 2 * core).astype(F32)
-    quarters = given.shape[0]
-    width = given.shape[2]
-
-    def swap_copy(q):
-        return remote(
-            given.at[q], taken.at[q], swap_send.at[q], swap_recv.at[q], partner
+    def return_copy(q):
+        return remote(
+            sent_back.at[q], got_back.at[q], return_send.at[q], return_recv.at[q], partner
         )
 
     for q in range(quarters):
-        given[q] = wide[:, q * width : (q + 1) * width].astype(BF)
-        swap_copy(q).start()
+        sent_back[q] = wide[:, q * width : (q + 1) * width].astype(BF)
+        return_copy(q).start()
     for q in range(quarters):
         at = slice(q * width, (q + 1) * width)
-        swap_copy(q).wait_recv()
-        mine, theirs = wide[:, at], taken[q].astype(F32)
+        return_copy(q).wait_recv()
+        mine, theirs = wide[:, at], got_back[q].astype(F32)
         band[:half, at] = (mine + theirs).astype(BF)
         band[half:, at] = ((mine - theirs) * sign).astype(BF)
 
@@ -511,7 +519,7 @@
             2 * there + core,
         )
 
-    lat_index = lax.broadcasted_iota(jnp.int32, (rows, points), 1).astype(F32)
+    lat_lane = lax.broadcasted_iota(jnp.int32, (rows, points), 1).astype(F32)
 
     def answer(group, carry):
         code = code_rows[group][:, :rows]
@@ -519,7 +527,7 @@
         lat = down_rows(lat // points, points) * points + down_rows(lat % points, points)
         one_hot = jnp.concatenate(
             [
-                jnp.where(lat == lat_index + float(c), 1.0, 0.0).astype(BF)
+                jnp.where(lat == lat_lane + float(c), 1.0, 0.0).astype(BF)
                 for c in range(0, 2 * half, points)
             ],
             axis=1,
@@ -567,7 +575,108 @@
 
     lax.fori_loop(1, TILES, finish_wave, 0)
     for q in range(quarters):
+        return_copy(q).wait_send()
+    def finish_chunk(slot, carry):
+        chunk_copy(slot).wait_send()
+        return carry
+
+    lax.fori_loop(1, CHIPS, finish_chunk, 0)
+    def finish_code(slot, carry):
+        code_copy(slot).wait_send()
+        return carry
+
+    lax.fori_loop(1, CHIPS, finish_code, 0)
+    for q in range(quarters):
         swap_copy(q).wait_send()
+        area_core(q).wait_send()
+    for step in range(1, ZS):
+        area_z(step).wait_send()
+    for step in range(1, XS):
+        area_x(step).wait_send()
+    for step in range(1, LEVS):
+        area_y(step).wait_send()
+
+
+    for way in range(2):
+        for piece in range(2):
+            give_tables(piece, way).wait_send()
+        pass_tables(way).wait_send()
+
+
+def regrid_call(chunks, codes, area_part, picks, wave_codes, wave_order, damping, legendre):
+    pairs, points = chunks.shape[1:]
+    room, width = codes.shape[2], area_part.shape[1]
+    lons, lats = LEVS * width, 2 * picks.shape[2]
+    half, share, groups = lats // 2, wave_codes.shape[1] // TILES, CHIPS // GROUP
+    slots, mixed = share // 2, CHIPS * share
+    order, back_order = slot_orders(slots)
+    vmem = pl.BlockSpec(memory_space=pltpu.VMEM)
+    smem = pl.BlockSpec(memory_space=pltpu.SMEM)
+    anywhere = pl.BlockSpec(memory_space=pl.ANY)
+    dma = pltpu.SemaphoreType.DMA
+    return pl.pallas_call(
+        regrid,
+        out_shape=jax.ShapeDtypeStruct((CHIPS, pairs, points), BF),
+        in_specs=[vmem] * 5 + [smem, vmem, anywhere, vmem, vmem],
+        out_specs=vmem,
+        scratch_shapes=[
+            pltpu.VMEM((CHIPS, pairs, points), BF),
+            pltpu.VMEM((CHIPS, 1, room), jnp.int32),
+            pltpu.VMEM((groups, 1, room), jnp.int32),
+            pltpu.VMEM((lats, lons), F32),
+            pltpu.VMEM((LEVS, 2, CHIPS, PAD_LAT, width), BF),
+            pltpu.VMEM((TILES * share, lons), BF),
+            pltpu.VMEM((2 * slots, half, half), BF),
+            pltpu.VMEM((slots, 2, CHIPS, half), F32),
+            pltpu.VMEM((LEVS, half, width), BF),
+            pltpu.VMEM((LEVS, half, width), BF),
+            pltpu.VMEM((half, lons), BF),
+            pltpu.VMEM((TILES, share, half), BF),
+            pltpu.VMEM((TILES, share, half), BF),
+            pltpu.VMEM((mixed, half), BF),
+            pltpu.VMEM((mixed, half), BF),
+            pltpu.VMEM((TILES, share, half), BF),
+            pltpu.VMEM((TILES, share, half), BF),
+            pltpu.VMEM((half, lons), F32),
+            pltpu.VMEM((LEVS, half, width), BF),
+            pltpu.VMEM((LEVS, half, width), BF),
+            pltpu.VMEM((lats, lons), BF),
+            pltpu.VMEM((CHIPS, pairs, points), BF),
+            dma((CHIPS,)),
+            dma((CHIPS,)),
+            dma((CHIPS,)),
+            dma((CHIPS,)),
+            dma((ZS + XS + 2 * LEVS,)),
+            dma((ZS + XS + 2 * LEVS,)),
+            dma((6,)),
+            dma((6,)),
+            dma((LEVS,)),
+            dma((LEVS,)),
+            dma((TILES,)),
+            dma((TILES,)),
+            dma((TILES,)),
+            dma((TILES,)),
+            dma((LEVS,)),
+            dma((LEVS,)),
+            dma((CHIPS,)),
+            dma((CHIPS,)),
+            dma((1,)),
+        ],
+        compiler_params=pltpu.CompilerParams(
+            collective_id=0, has_side_effects=True, vmem_limit_bytes=VMEM_LIMIT
+        ),
+    )(
+        chunks,
+        codes,
+        area_part,
+        picks,
+        wave_codes,
+        wave_order,
+        damping,
+        legendre,
+        order,
+        back_order,
+    )
 
 
 def slot_orders(slots):
@@ -615,10 +724,7 @@
     lats = lat_dev * TILES
     half = lats // 2
     slots = wave_order.shape[0] // TILES
-    own_slots = legendre.shape[0]
-    share = 2 * slots
     width = lons // levs
-    groups = CHIPS // GROUP
 
     lat = pair_owner * lat_dev + pair_block // per_row
     row = jnp.where(lat < half, lat, lats + half - 1 - lat)
@@ -633,10 +739,6 @@
     part = lax.dynamic_slice_in_dim(band_area, lev * width, width, axis=1)
     part = (own_weight[:, None] / part).astype(BF)
     area_part = jnp.pad(part, ((0, PAD_LAT - lat_dev), (0, 0)))
-    tables = lax.all_gather(
-        legendre.reshape(own_slots * 2 * half, half), "lev", axis=0, tiled=True
-    ).reshape(slots, 2, half, half)
-
     margin_q = margin.reshape(blocks, 2, cells, points)
     chunks = jnp.einsum(
         "fbc,bkcg->fbkg",
@@ -646,102 +748,18 @@
     )
     chunks = chunks.astype(BF).reshape(fields, pairs, points)
 
-    parts = jnp.arange(2, dtype=jnp.int32)[None, :, None] * 1024
-    wave_rows = (wave_order.reshape(TILES, 1, slots) + parts).reshape(-1, 1)
-    wave_rows = jnp.broadcast_to(wave_rows, (TILES * share, points))
-
-    waves = lax.dynamic_slice_in_dim(wave_order, tile * slots, slots)
-    damping = lax.dynamic_slice_in_dim(diffusion, lev * fields, fields)
-    degree = (
-        waves[:, None, None]
-        + 2 * jnp.arange(half, dtype=jnp.int32)[None, None, :]
-        + jnp.arange(2, dtype=jnp.int32)[None, :, None]
-    )
-    growth = (degree * (degree + 1)).astype(F32) / float(TRUNC * (TRUNC + 1))
-    doubled = jnp.where(waves == 0, 1.0, 2.0).astype(F32)[:, None, None, None]
-    response = jnp.where(
-        (degree <= TRUNC)[:, :, None, :],
-        doubled / (1.0 + damping[None, None, :, None] * growth[:, :, None, :]),
-        0.0,
-    )
-
-    vmem = pl.BlockSpec(memory_space=pltpu.VMEM)
-    anywhere = pl.BlockSpec(memory_space=pl.ANY)
-    dma = pltpu.SemaphoreType.DMA
-    spectra, table, code_rows = pl.pallas_call(
-        to_spectra,
-        out_shape=(
-            jax.ShapeDtypeStruct((TILES, share, half), BF),
-            jax.ShapeDtypeStruct((TILES * share, lons), BF),
-            jax.ShapeDtypeStruct((groups, 1, room), jnp.int32),
-        ),
-        in_specs=[vmem] * 5,
-        out_specs=(vmem, anywhere, vmem),
-        scratch_shapes=[
-            pltpu.VMEM((CHIPS, pairs, points), BF),
-            pltpu.VMEM((CHIPS, 1, room), jnp.int32),
-            pltpu.VMEM((lats, lons), F32),
-            pltpu.VMEM((levs, 2, CHIPS, PAD_LAT, width), BF),
-            pltpu.VMEM((TILES * share, lons), BF),
-            pltpu.VMEM((levs, half, width), BF),
-            pltpu.VMEM((levs, half, width), BF),
-            pltpu.VMEM((half, lons), BF),
-            pltpu.VMEM((TILES, share, half), BF),
-            dma((CHIPS,)),
-            dma((CHIPS,)),
-            dma((levs,)),
-            dma((levs,)),
-            dma((TILES,)),
-            dma((TILES,)),
-            dma((CHIPS,)),
-            dma((CHIPS,)),
-            dma((ZS + XS + 2 * LEVS,)),
-            dma((ZS + XS + 2 * LEVS,)),
-            dma((2,)),
-        ],
-        compiler_params=pltpu.CompilerParams(
-            collective_id=0, has_side_effects=True, vmem_limit_bytes=VMEM_LIMIT
-        ),
-    )(chunks, codes, area_part, lat_picks(lat_dev, half), wave_rows)
-
-    order, back_order = slot_orders(slots)
-    mixed = CHIPS * share
-    replies = pl.pallas_call(
-        from_spectra,
-        out_shape=jax.ShapeDtypeStruct((CHIPS, pairs, points), BF),
-        in_specs=[vmem, vmem, vmem, anywhere, vmem, anywhere, vmem],
-        out_specs=vmem,
-        scratch_shapes=[
-            pltpu.VMEM((slots, 2, half, half), BF),
-            pltpu.VMEM((TILES * share, lons), BF),
-            pltpu.VMEM((2, mixed, half), BF),
-            pltpu.VMEM((2, mixed, half), BF),
-            pltpu.VMEM((TILES, share, half), BF),
-            pltpu.VMEM((TILES, share, half), BF),
-            pltpu.VMEM((half, lons), F32),
-            pltpu.VMEM((levs, half, width), BF),
-            pltpu.VMEM((levs, half, width), BF),
-            pltpu.VMEM((lats, lons), BF),
-            pltpu.VMEM((CHIPS, pairs, points), BF),
-            dma((TILES,)),
-            dma((TILES,)),
-            dma((levs,)),
-            dma((levs,)),
-            dma((CHIPS,)),
-            dma((CHIPS,)),
-            dma((2,)),
-        ],
-        compiler_params=pltpu.CompilerParams(
-            collective_id=1, has_side_effects=True, vmem_limit_bytes=VMEM_LIMIT
-        ),
-    )(
-        spectra.reshape(2, mixed, half),
-        order,
-        back_order,
-        tables,
-        response,
-        table,
-        code_rows,
+    part_codes = jnp.arange(2, dtype=jnp.int32)[None, :, None] * 1024
+    wave_codes = (wave_order.reshape(TILES, 1, slots) + part_codes).reshape(1, -1)
+    damping = lax.dynamic_slice_in_dim(diffusion, lev * fields, fields)[:, None]
+    replies = regrid_call(
+        chunks,
+        codes,
+        area_part,
+        lat_picks(lat_dev, half),
+        wave_codes,
+        wave_order,
+        damping,
+        legendre.reshape(-1, half, half),
     )
 
     cube = jnp.einsum(

time: 225 us -> 194 us (0.86)
  Pallas kernels: 198 us -> 179 us
  between operations: 13.6 us -> 0.09 us
    pallas_call x2 -> x1, Pallas kernels: 198 us -> 179 us  [regrid_call(): pl.pallas_call(regrid, out_shape=jax.ShapeDtypeStruct((CHIPS, pairs, poin...]
  transfers between devices with their start and end apart: 1 -> 0, of which waited for: 0 -> 0; matrix products, arithmetic and copies ran while one was open for 4% -> 0% of each run, Pallas kernels for 49% -> 0%
where the time goes in v1:
time: 194 us; the launch traced here: 193 us
  Pallas kernels  179 us (92%)
  local copies, waits for them, and re-layouts  9.09 us (5%)
  matrix products  2.47 us (1%)
  other arithmetic  2.23 us (1%)
    pallas_call x1, Pallas kernels, regrid_call(): pl.pallas_call(regrid, out_shape=jax.ShapeDtypeStruct((CHIPS, pairs, poin...  179 us

profile of v1, /device:TPU:1, one launch (start us, length us, event | category | flops | bytes accessed | tf_op | source)
XLA Modules:
  0.0 193.0 jit_solution(4876149007486190113)
XLA Ops:
  0.0 0.0 copy-start
  0.0 1.5 gather_fusion
  1.5 0.8 divide_convert_fusion.1
  2.3 0.6 pad.24.area_part
  2.9 0.7 fusion.8
  3.7 0.1 fusion.11
  3.8 0.6 pad_add_fusion.codes
  4.4 0.7 dynamic-slice_bitcast_fusion
  5.1 0.7 copy.20.damping
  5.8 0.0 copy-done
  5.8 1.3 reshape.76
  7.1 0.5 fusion
  7.6 0.0 copy-start.2
  7.6 1.9 copy.19
  9.5 0.0 copy-done.2
  9.5 0.1 add.84
  9.6 0.1 broadcast_add_fusion
  9.7 0.7 add.88.wave_codes
  10.5 0.0 copy-start.1
  10.5 179.1 %shard_map.127 = bf16[32,144,128]{2,1,0:T(8,128)(2,1)} custom-call(bf16[32,144,128]{2,1,0:T(8,128)(2,1)} %bitcast.24, s32[4,1,640]{2,1,0:T(1,128)} %pad_add_fusion.codes, bf16[16,384]{1,0:T(8,128)(2,1)} %pad.24.area_part, bf16[2,2,384,256]{3,2,1,0:T(8,128)(2,1)} %constant.58.clone.pick_rows, s32[1,1536]{1,0:T(1,128)} %add.88.wave_codes, s32[768]{0:T(1024)} %wave_order.1, ...), custom_call_target="tpu_custom_call" | custom-call | tf_op jit(solution)/shard_map/pallas_call | solution.py:617
  189.5 0.0 copy-done.1
  189.6 0.1 div.28
  189.6 2.0 %fusion.4 = bf16[32,72,64]{2,0,1:T(8,128)(2,1)S(1)} fusion(bf16[72,2,64,128]{3,2,1,0:T(8,128)(2,1)S(1)} %bitcast.23, bf16[32,72,2,128]{3,2,1,0:T(2,128)(2,1)} %bitcast.27, f32[72,64]{1,0:T(8,128)S(1)} %div.28), kind=kOutput, calls=%fused_computation.6 | convolution fusion | flops 75792384 | bytes 3852288 | tf_op jit(solution)/shard_map/fbkg,bkcg->fbc/dot_general | solution.py:765
  191.6 0.2 copy.22
  191.9 1.1 reshape.80
  (7 shorter events, 0.0 us)
Async XLA Ops:
  0.0 5.8 %copy-start = (bf16[144,64,128]{2,1,0:T(8,128)(2,1)S(1)}, bf16[144,64,128]{2,1,0:T(8,128)(2,1)}, u32[]{:S(2)}) copy-start(bf16[144,64,128]{2,1,0:T(8,128)(2,1)} %param.14) | copy-start | bytes 7077892
  7.6 1.9 %copy-start.2 = (s32[768]{0:T(1024)S(1)}, s32[768]{0:T(1024)}, u32[]{:S(2)}) copy-start(s32[768]{0:T(1024)} %wave_order.1) | copy-start | bytes 9220
  10.5 179.1 %copy-start.1 = (f32[4608]{0:T(1024)S(1)}, f32[4608]{0:T(1024)}, u32[]{:S(2)}) copy-start(f32[4608]{0:T(1024)} %param.17) | copy-start | bytes 55300

commit v2 on v1

--- a/solution.py
+++ b/solution.py
@@ -14,6 +14,7 @@
 BF = jnp.bfloat16
 F32 = jnp.float32
 GROUP = 4
+WINDOW = 3
 PAD_LAT = 16
 VMEM_LIMIT = 56 * 2**20
 NT = (((1,), (1,)), ((), ()))
@@ -61,6 +62,15 @@
     )
 
 
+def drain(ref, sem):
+    pltpu.make_async_copy(ref, ref, sem).wait()
+
+
+def offset(slot):
+    k = slot % ZS
+    return slot // ZS, (k + 1) // 2 * (2 * (k % 2) - 1)
+
+
 def slot_of(tile):
     return (tile % 2) * CHIPS + tile // 2
 
@@ -97,7 +107,8 @@
     chunks,
     codes,
     area_part,
-    pick_rows,
+    pack_rows,
+    unmix,
     wave_codes,
     wave_order,
     damping,
@@ -109,13 +120,14 @@
     code_in,
     code_rows,
     totals,
+    area_in,
     area,
     table,
     tables,
     response,
     given,
     taken,
-    folded,
+    turned,
     fourier,
     spectra,
     sorted_in,
@@ -158,29 +170,28 @@
     per_row = lons // points
     greet()
 
-    area[lev, core, chip] = area_part[...]
+    area_in[chip] = area_part[...]
 
     def area_z(step):
         there = chip_at(x, z + step)
-        here = area.at[lev, core, chip]
-        sems = area_send.at[step], area_recv.at[step]
+        here = area_in.at[chip]
+        sems = area_send.at[0], area_recv.at[0]
         return remote(here, here, *sems, 2 * there + core)
 
     def area_x(step):
         there = chip_at(x + step, z)
-        here = area.at[lev, core, pl.ds(pl.multiple_of(x * ZS, ZS), ZS)]
-        sems = area_send.at[ZS + step], area_recv.at[ZS + step]
+        here = area_in.at[pl.ds(pl.multiple_of(x * ZS, ZS), ZS)]
+        sems = area_send.at[1], area_recv.at[1]
         return remote(here, here, *sems, 2 * there + core)
 
     def area_y(step):
         here = area.at[lev, core]
-        sems = area_send.at[ZS + XS + step], area_recv.at[ZS + XS + step]
+        sems = area_send.at[2], area_recv.at[2]
         return remote(here, here, *sems, tile, (lev + step) % LEVS)
 
     def area_core(q):
         here = area.at[q, core]
-        at = ZS + XS + LEVS + q
-        return remote(here, here, area_send.at[at], area_recv.at[at], partner)
+        return remote(here, here, area_send.at[3], area_recv.at[3], partner)
 
     for step in range(1, ZS):
         area_z(step).start()
@@ -194,13 +205,12 @@
     keep_tables.start()
 
     def give_tables(piece, way):
-        first, count = ((0, own // 3), (own // 3, own - own // 3))[piece]
-        at = 2 * piece + way
+        first, count = ((0, own // 6), (own // 6, own - own // 6))[piece]
         return remote(
             legendre.at[pl.ds(first, count)],
             own_tables(first, count),
-            table_send.at[at],
-            table_recv.at[at],
+            table_send.at[0],
+            table_recv.at[way],
             tile,
             (lev + (1, LEVS - 1)[way]) % LEVS,
         )
@@ -211,8 +221,8 @@
         return remote(
             here,
             here,
-            table_send.at[4 + way],
-            table_recv.at[4 + way],
+            table_send.at[0],
+            table_recv.at[2],
             tile,
             (lev + (1, LEVS - 1)[way]) % LEVS,
         )
@@ -221,12 +231,13 @@
         give_tables(0, way).start()
 
     def code_copy(slot):
-        there = chip_at(x + slot // ZS, z + slot % ZS)
+        dx, dz = offset(slot)
+        there = chip_at(x + dx, z + dz)
         return remote(
             codes.at[slot % GROUP],
             code_in.at[slot],
-            code_send.at[slot],
-            code_recv.at[slot],
+            code_send.at[0],
+            code_recv.at[slot // GROUP],
             2 * there + core,
         )
 
@@ -238,12 +249,13 @@
     code_in[0] = codes[0]
 
     def chunk_copy(slot):
-        there = chip_at(x + slot // ZS, z + slot % ZS)
+        dx, dz = offset(slot)
+        there = chip_at(x + dx, z + dz)
         return remote(
             chunks.at[there],
             arrived.at[slot],
-            chunk_send.at[slot],
-            chunk_recv.at[slot],
+            chunk_send.at[0],
+            chunk_recv.at[slot // GROUP],
             2 * there + core,
         )
 
@@ -251,8 +263,26 @@
         chunk_copy(slot).start()
         return carry
 
-    lax.fori_loop(1, CHIPS, start_chunk, 0)
+    lax.fori_loop(1, WINDOW * GROUP, start_chunk, 0)
     arrived[0] = chunks[chip]
+
+    slots = response.shape[0]
+
+    def make_response(slot, carry):
+        wave = wave_order[tile * slots + slot]
+        doubled = jnp.where(wave == 0, 1.0, 2.0).astype(F32)
+        for p in range(2):
+            degree = wave + p + 2 * lax.broadcasted_iota(jnp.int32, (1, half), 1)
+            growth = (degree * (degree + 1)).astype(F32) * (1.0 / (TRUNC * (TRUNC + 1)))
+            value = doubled / (1.0 + damping[...] * growth)
+            response[slot, p] = jnp.where(degree <= TRUNC, value, 0.0)
+        return carry
+
+    lax.fori_loop(0, slots, make_response, 0)
+
+    drain(area_in.at[pl.ds(0, ZS - 1)], area_recv.at[0])
+    for step in range(1, XS):
+        area_x(step).start()
 
     strip = points
     longitude = lax.broadcasted_iota(jnp.int32, (strip, points), 1)
@@ -274,38 +304,35 @@
 
     lax.fori_loop(0, table.shape[0] // strip, make_rows, 0)
 
-    for step in range(1, ZS):
-        area_z(step).wait_recv()
-    for step in range(1, XS):
-        area_x(step).start()
-
-    slots = response.shape[0]
-
-    def make_response(slot, carry):
-        wave = wave_order[tile * slots + slot]
-        doubled = jnp.where(wave == 0, 1.0, 2.0).astype(F32)
-        for p in range(2):
-            degree = wave + p + 2 * lax.broadcasted_iota(jnp.int32, (1, half), 1)
-            growth = (degree * (degree + 1)).astype(F32) * (1.0 / (TRUNC * (TRUNC + 1)))
-            value = doubled / (1.0 + damping[...] * growth)
-            response[slot, p] = jnp.where(degree <= TRUNC, value, 0.0)
-        return carry
-
-    lax.fori_loop(0, slots, make_response, 0)
+    drain(area_in.at[pl.ds(0, CHIPS - ZS)], area_recv.at[1])
+    area[lev, core] = jnp.dot(
+        pack_rows[...], area_in[...].reshape(CHIPS * PAD_LAT, -1), preferred_element_type=F32
+    ).astype(BF)
+    area_core(lev).start()
+    for step in range(1, LEVS):
+        area_y(step).start()
+    for way in range(2):
+        give_tables(1, way).start()
 
     lat_index = lax.broadcasted_iota(jnp.int32, (lats, rows), 0)
 
     def add_group(group, first):
-        for j in range(GROUP):
-            if not (first and j == 0):
-                code_copy(group * GROUP + j).wait_recv()
-                chunk_copy(group * GROUP + j).wait_recv()
+        ahead = group + WINDOW
+
+        @pl.when(ahead < CHIPS // GROUP)
+        def _():
+            for j in range(GROUP):
+                chunk_copy(ahead * GROUP + j).start()
+
+        from_slot = pl.ds(1, GROUP - 1) if first else pl.ds(group * GROUP, GROUP)
+        drain(code_in.at[from_slot], code_recv.at[group])
+        drain(arrived.at[from_slot], chunk_recv.at[group])
         code = code_in[group * GROUP]
         for j in range(1, GROUP):
             code = code + code_in[group * GROUP + j]
         code_rows[group] = code
         code = code[:, :rows]
-        one_hot = jnp.where(lat_index == code // 16, 1.0, 0.0).astype(BF)
+        one_hot = jnp.where(lat_index == code // 16384, 1.0, 0.0).astype(BF)
         values = arrived[pl.ds(group * GROUP, GROUP)].reshape(rows, points)
         where = down_rows(code % 16, points).astype(BF)
         for b in range(0, per_row, 2):
@@ -325,36 +352,24 @@
         return carry
 
     add_group(0, True)
-    for step in range(1, XS):
-        area_x(step).wait_recv()
+    lax.fori_loop(1, 4, later_group, 0)
+    drain(area.at[pl.ds(0, LEVS - 1), core], area_recv.at[2])
     for step in range(1, LEVS):
-        area_y(step).start()
-    for way in range(2):
-        give_tables(1, way).start()
-    lax.fori_loop(1, 4, later_group, 0)
-    for step in range(1, LEVS):
-        area_y(step).wait_recv()
-    for q in range(LEVS):
-        area_core(q).start()
+        area_core((lev + step) % LEVS).start()
     lax.fori_loop(4, CHIPS // GROUP, later_group, 0)
-    for q in range(LEVS):
-        area_core(q).wait_recv()
+    drain(area.at[:, core], area_recv.at[3])
 
     sign = (1 - 2 * core).astype(F32)
     quarters = LEVS
     width = lons // LEVS
 
     def weights(q, side):
-        found = []
-        for c in range(2):
-            part = area[q, c, side * (CHIPS // 2) : (side + 1) * (CHIPS // 2)]
-            part = part.reshape(-1, width)
-            found.append(jnp.dot(pick_rows[side, c], part, preferred_element_type=F32))
-        return found[0] + found[1]
+        at = slice(side * (half // 2), (side + 1) * (half // 2))
+        return jnp.concatenate([area[q, c ^ side, at].astype(F32) for c in range(2)], axis=0)
 
     def swap_copy(q):
         return remote(
-            given.at[q], taken.at[q], swap_send.at[q], swap_recv.at[q], partner
+            given.at[q], taken.at[q], swap_send.at[0], swap_recv.at[q], partner
         )
 
     for q in range(quarters):
@@ -367,63 +382,57 @@
     for q in range(quarters):
         at = slice(q * width, (q + 1) * width)
         swap_copy(q).wait_recv()
-        folded[:, at] = (totals[:half, at] + taken[q].astype(F32)).astype(BF)
+        folded = (totals[:half, at] + taken[q].astype(F32)).astype(BF)
+        turned[at, :] = lax.dot_general(
+            folded, unmix[...], TN, preferred_element_type=F32
+        ).astype(BF)
 
     share = fourier.shape[1]
-    batch = ZS
+    batch = 2 * ZS
 
     def fourier_copy(peer):
         return remote(
             fourier.at[peer],
             spectra.at[slot_of(tile)],
-            fourier_send.at[peer],
-            fourier_recv.at[tile],
+            fourier_send.at[0],
+            fourier_recv.at[0],
             peer,
         )
 
     def transform(step, carry):
-        first = ((x + step // 2) % XS) * (2 * ZS) + ((z // (ZS // 2) + step) % 2) * batch
+        first = ((x + step) % XS) * batch
         at = pl.ds(pl.multiple_of(first * share, batch * share), batch * share)
-        part = lax.dot_general(table[at, :], folded[...], NT, preferred_element_type=F32)
+        part = jnp.dot(table[at, :], turned[...], preferred_element_type=F32)
         fourier[pl.ds(first, batch)] = part.astype(BF).reshape(batch, share, half)
-        for j in range(batch):
-            peer = first + j
+
+        def start_one(j, carry):
+            _, dz = offset(j // 2)
+            peer = first + (z + dz + ZS) % ZS * 2 + (core + j) % 2
 
             @pl.when(peer != tile)
             def _():
                 fourier_copy(peer).start()
 
+            return carry
+
+        lax.fori_loop(0, batch, start_one, 0)
         return carry
 
-    lax.fori_loop(0, TILES // batch, transform, 0)
+    lax.fori_loop(0, XS, transform, 0)
     spectra[slot_of(tile)] = fourier[tile]
     for way in range(2):
-        for piece in range(2):
-            give_tables(piece, way).wait_recv()
+        drain(tables.at[pl.ds(0, own)], table_recv.at[way])
         pass_tables(way).start()
 
-    def finish_fourier(step, carry):
-        peer = (tile + step) % TILES
-        fourier_copy(peer).wait_send()
-        remote(
-            fourier.at[peer],
-            spectra.at[slot_of(peer)],
-            fourier_send.at[peer],
-            fourier_recv.at[peer],
-            peer,
-        ).wait_recv()
-        return carry
-
-    lax.fori_loop(1, TILES, finish_fourier, 0)
+    drain(spectra.at[pl.ds(0, TILES - 1)], fourier_recv.at[0])
 
     def wave_copy(peer):
         return remote(
-            parts.at[peer], returned.at[tile], wave_send.at[peer], wave_recv.at[tile], peer
+            parts.at[peer], returned.at[tile], wave_send.at[0], wave_recv.at[x], peer
         )
 
     mixed = 2 * CHIPS
-    for way in range(2):
-        pass_tables(way).wait_recv()
+    drain(tables.at[pl.ds(0, own)], table_recv.at[2])
     keep_tables.wait()
     for p in range(2):
         rows_in = spectra[p * CHIPS : (p + 1) * CHIPS].reshape(CHIPS * share, half)
@@ -452,40 +461,33 @@
             part = jnp.dot(back_order[at, :], sorted_out[...], preferred_element_type=F32)
             part = part.astype(BF).reshape(ZS, share, half)
             for j in range(ZS):
-                peer = 2 * (first + j) + p
-                parts[peer] = part[j]
+                parts[2 * (first + j) + p] = part[j]
+
+            def start_one(j, carry):
+                _, dz = offset(j)
+                peer = 2 * (first + (z + dz + ZS) % ZS) + p
 
                 @pl.when(peer != tile)
                 def _():
                     wave_copy(peer).start()
 
+                return carry
+
+            lax.fori_loop(0, ZS, start_one, 0)
             return carry
 
         lax.fori_loop(0, XS, send_back, 0)
     returned[tile] = parts[tile]
 
-    def wave_arrival(peer):
-        return remote(
-            parts.at[peer], returned.at[peer], wave_send.at[peer], wave_recv.at[peer], peer
-        )
-
     def inverse(step):
-        first = ((x + XS - step) % XS) * (2 * ZS)
-
-        def wait_one(j, carry):
-            @pl.when(first + j != tile)
-            def _():
-                wave_arrival(first + j).wait_recv()
-
-            return carry
-
-        lax.fori_loop(0, 2 * ZS, wait_one, 0)
-        values = returned[pl.ds(first, 2 * ZS)].reshape(2 * ZS * share, half)
+        there = (x + XS - step) % XS
+        first = there * (2 * ZS)
+        count = 2 * ZS - 1 if step == 0 else 2 * ZS
+        drain(returned.at[pl.ds(0, count)], wave_recv.at[there])
+        values = returned[pl.ds(first, 2 * ZS)].reshape(2 * ZS * share, half).T
         at = pl.ds(pl.multiple_of(first * share, 2 * ZS * share), 2 * ZS * share)
         for c in range(0, lons, 512):
-            term = lax.dot_general(
-                values, table[at, c : c + 512], TN, preferred_element_type=F32
-            )
+            term = jnp.dot(values, table[at, c : c + 512], preferred_element_type=F32)
             if step == 0:
                 wide[:, c : c + 512] = term
             else:
@@ -496,7 +498,7 @@
 
     def return_copy(q):
         return remote(
-            sent_back.at[q], got_back.at[q], return_send.at[q], return_recv.at[q], partner
+            sent_back.at[q], got_back.at[q], return_send.at[0], return_recv.at[q], partner
         )
 
     for q in range(quarters):
@@ -510,12 +512,13 @@
         band[half:, at] = ((mine - theirs) * sign).astype(BF)
 
     def pair_copy(slot):
-        there = chip_at(x - slot // ZS, z - slot % ZS)
+        dx, dz = offset(slot)
+        there = chip_at(x - dx, z - dz)
         return remote(
             picked.at[slot],
             replies.at[chip],
-            pair_send.at[slot],
-            pair_recv.at[chip],
+            pair_send.at[0],
+            pair_recv.at[0],
             2 * there + core,
         )
 
@@ -523,7 +526,7 @@
 
     def answer(group, carry):
         code = code_rows[group][:, :rows]
-        lat = code // 16
+        lat = code // 16 % 1024
         lat = down_rows(lat // points, points) * points + down_rows(lat % points, points)
         one_hot = jnp.concatenate(
             [
@@ -555,61 +558,29 @@
     lax.fori_loop(0, CHIPS // GROUP, answer, 0)
     replies[chip] = picked[0]
 
-    def finish_pair(slot, carry):
-        pair_copy(slot).wait_send()
-        here = chip_at(x - slot // ZS, z - slot % ZS)
-        remote(
-            picked.at[slot],
-            replies.at[here],
-            pair_send.at[slot],
-            pair_recv.at[here],
-            2 * here + core,
-        ).wait_recv()
-        return carry
-
-    lax.fori_loop(1, CHIPS, finish_pair, 0)
-
-    def finish_wave(step, carry):
-        wave_copy((tile + step) % TILES).wait_send()
-        return carry
-
-    lax.fori_loop(1, TILES, finish_wave, 0)
-    for q in range(quarters):
-        return_copy(q).wait_send()
-    def finish_chunk(slot, carry):
-        chunk_copy(slot).wait_send()
-        return carry
-
-    lax.fori_loop(1, CHIPS, finish_chunk, 0)
-    def finish_code(slot, carry):
-        code_copy(slot).wait_send()
-        return carry
-
-    lax.fori_loop(1, CHIPS, finish_code, 0)
-    for q in range(quarters):
-        swap_copy(q).wait_send()
-        area_core(q).wait_send()
-    for step in range(1, ZS):
-        area_z(step).wait_send()
-    for step in range(1, XS):
-        area_x(step).wait_send()
-    for step in range(1, LEVS):
-        area_y(step).wait_send()
-
-
-    for way in range(2):
-        for piece in range(2):
-            give_tables(piece, way).wait_send()
-        pass_tables(way).wait_send()
-
-
-def regrid_call(chunks, codes, area_part, picks, wave_codes, wave_order, damping, legendre):
+    drain(replies.at[pl.ds(0, CHIPS - 1)], pair_recv.at[0])
+    drain(picked.at[pl.ds(0, CHIPS - 1)], pair_send.at[0])
+    drain(parts.at[pl.ds(0, TILES - 1)], wave_send.at[0])
+    drain(sent_back, return_send.at[0])
+    drain(fourier.at[pl.ds(0, TILES - 1)], fourier_send.at[0])
+    drain(given, swap_send.at[0])
+    drain(chunks.at[pl.ds(0, CHIPS - 1)], chunk_send.at[0])
+    drain(code_in.at[pl.ds(0, CHIPS - 1)], code_send.at[0])
+    drain(area_in.at[pl.ds(0, ZS - 1)], area_send.at[0])
+    drain(area_in.at[pl.ds(0, CHIPS - ZS)], area_send.at[1])
+    drain(area.at[pl.ds(0, LEVS - 1), core], area_send.at[2])
+    drain(area.at[:, core], area_send.at[3])
+    drain(tables.at[pl.ds(0, 3 * own)], table_send.at[0])
+
+
+def regrid_call(chunks, codes, area_part, lat_dev, wave_codes, wave_order, damping, legendre):
     pairs, points = chunks.shape[1:]
     room, width = codes.shape[2], area_part.shape[1]
-    lons, lats = LEVS * width, 2 * picks.shape[2]
+    lons, lats = LEVS * width, lat_dev * TILES
     half, share, groups = lats // 2, wave_codes.shape[1] // TILES, CHIPS // GROUP
     slots, mixed = share // 2, CHIPS * share
     order, back_order = slot_orders(slots)
+    pack_rows, unmix = lat_orders(lat_dev)
     vmem = pl.BlockSpec(memory_space=pltpu.VMEM)
     smem = pl.BlockSpec(memory_space=pltpu.SMEM)
     anywhere = pl.BlockSpec(memory_space=pl.ANY)
@@ -617,20 +588,21 @@
     return pl.pallas_call(
         regrid,
         out_shape=jax.ShapeDtypeStruct((CHIPS, pairs, points), BF),
-        in_specs=[vmem] * 5 + [smem, vmem, anywhere, vmem, vmem],
+        in_specs=[vmem] * 6 + [smem, vmem, anywhere, vmem, vmem],
         out_specs=vmem,
         scratch_shapes=[
             pltpu.VMEM((CHIPS, pairs, points), BF),
             pltpu.VMEM((CHIPS, 1, room), jnp.int32),
             pltpu.VMEM((groups, 1, room), jnp.int32),
             pltpu.VMEM((lats, lons), F32),
-            pltpu.VMEM((LEVS, 2, CHIPS, PAD_LAT, width), BF),
+            pltpu.VMEM((CHIPS, PAD_LAT, width), BF),
+            pltpu.VMEM((LEVS, 2, half, width), BF),
             pltpu.VMEM((TILES * share, lons), BF),
             pltpu.VMEM((2 * slots, half, half), BF),
             pltpu.VMEM((slots, 2, CHIPS, half), F32),
             pltpu.VMEM((LEVS, half, width), BF),
             pltpu.VMEM((LEVS, half, width), BF),
-            pltpu.VMEM((half, lons), BF),
+            pltpu.VMEM((lons, half), BF),
             pltpu.VMEM((TILES, share, half), BF),
             pltpu.VMEM((TILES, share, half), BF),
             pltpu.VMEM((mixed, half), BF),
@@ -642,24 +614,24 @@
             pltpu.VMEM((LEVS, half, width), BF),
             pltpu.VMEM((lats, lons), BF),
             pltpu.VMEM((CHIPS, pairs, points), BF),
-            dma((CHIPS,)),
-            dma((CHIPS,)),
-            dma((CHIPS,)),
-            dma((CHIPS,)),
-            dma((ZS + XS + 2 * LEVS,)),
-            dma((ZS + XS + 2 * LEVS,)),
-            dma((6,)),
-            dma((6,)),
+            dma((1,)),
+            dma((groups,)),
+            dma((1,)),
+            dma((groups,)),
+            dma((4,)),
+            dma((4,)),
+            dma((1,)),
+            dma((3,)),
+            dma((1,)),
             dma((LEVS,)),
+            dma((1,)),
+            dma((1,)),
+            dma((1,)),
+            dma((XS,)),
+            dma((1,)),
             dma((LEVS,)),
-            dma((TILES,)),
-            dma((TILES,)),
-            dma((TILES,)),
-            dma((TILES,)),
-            dma((LEVS,)),
-            dma((LEVS,)),
-            dma((CHIPS,)),
-            dma((CHIPS,)),
+            dma((1,)),
+            dma((1,)),
             dma((1,)),
         ],
         compiler_params=pltpu.CompilerParams(
@@ -669,7 +641,8 @@
         chunks,
         codes,
         area_part,
-        picks,
+        pack_rows,
+        unmix,
         wave_codes,
         wave_order,
         damping,
@@ -690,15 +663,24 @@
     return jnp.asarray(order, BF), jnp.asarray(order.T.copy(), BF)
 
 
-def lat_picks(lat_dev, half):
-    picks = np.zeros((2, 2, half, CHIPS // 2 * PAD_LAT), np.float32)
-    for tile in range(TILES):
+def mixed_row(lat, lat_dev):
+    tile = lat // lat_dev
+    return tile % 2 * (CHIPS // 2 * lat_dev) + tile // 2 * lat_dev + lat % lat_dev
+
+
+def lat_orders(lat_dev):
+    quarter = CHIPS // 2 * lat_dev
+    pack = np.zeros((2 * quarter, CHIPS * PAD_LAT), np.float32)
+    for chip in range(CHIPS):
         for i in range(lat_dev):
-            lat = tile * lat_dev + i
-            side = int(lat >= half)
-            to = lat if side == 0 else 2 * half - 1 - lat
-            picks[side, tile % 2, to, (tile // 2) % (CHIPS // 2) * PAD_LAT + i] = 1.0
-    return jnp.asarray(picks, BF)
+            row = chip * lat_dev + i
+            if chip >= CHIPS // 2:
+                row = quarter + (CHIPS - 1 - chip) * lat_dev + lat_dev - 1 - i
+            pack[row, chip * PAD_LAT + i] = 1.0
+    unmix = np.zeros((2 * quarter, 2 * quarter), np.float32)
+    lats = np.arange(2 * quarter)
+    unmix[mixed_row(lats, lat_dev), lats] = 1.0
+    return jnp.asarray(pack, BF), jnp.asarray(unmix, BF)
 
 
 def shards(
@@ -727,8 +709,10 @@
     width = lons // levs
 
     lat = pair_owner * lat_dev + pair_block // per_row
-    row = jnp.where(lat < half, lat, lats + half - 1 - lat)
-    code = row * 16 + pair_block % per_row
+    south = jnp.where(lat < half, 0, half)
+    north = jnp.where(lat < half, lat, lats - 1 - lat)
+    code = (south + mixed_row(north, lat_dev)) * 1024 + south + north
+    code = code * 16 + pair_block % per_row
     room = -(-GROUP * pairs // points) * points
     codes = jnp.stack(
         [jnp.pad(code, (j * pairs, room - (j + 1) * pairs))[None] for j in range(GROUP)]
@@ -755,7 +739,7 @@
         chunks,
         codes,
         area_part,
-        lat_picks(lat_dev, half),
+        lat_dev,
         wave_codes,
         wave_order,
         damping,

time: 194 us -> 177 us (0.912)
  Pallas kernels: 179 us -> 161 us
    pallas_call x1, Pallas kernels: 179 us -> 161 us  [regrid_call(): pl.pallas_call(regrid, out_shape=jax.ShapeDtypeStruct((CHIPS, pairs, poin...]
where the time goes in v2:
time: 177 us; the launch traced here: 175 us
  Pallas kernels  161 us (91%)
  local copies, waits for them, and re-layouts  9.09 us (5%)
  matrix products  2.47 us (1%)
  other arithmetic  2.26 us (1%)
    pallas_call x1, Pallas kernels, regrid_call(): pl.pallas_call(regrid, out_shape=jax.ShapeDtypeStruct((CHIPS, pairs, poin...  161 us

profile of v2, /device:TPU:1, one launch (start us, length us, event | category | flops | bytes accessed | tf_op | source)
XLA Modules:
  0.0 174.9 jit_solution(8019136402654829067)
XLA Ops:
  0.0 0.0 copy-start
  0.0 1.5 gather_fusion
  1.5 0.8 divide_convert_fusion.1
  2.3 0.6 pad.24.area_part
  2.9 0.7 fusion.11
  3.7 0.1 fusion.13
  3.8 0.6 pad_add_fusion.codes
  4.4 0.7 dynamic-slice_bitcast_fusion
  5.1 0.7 copy.21.damping
  5.8 0.0 copy-done
  5.8 1.3 reshape.76
  7.1 0.5 fusion
  7.6 0.0 copy-start.2
  7.6 1.9 %copy.20 = bf16[32,72,2,128]{3,2,1,0:T(2,128)(2,1)} copy(bf16[32,72,2,128]{3,0,2,1:T(8,128)(2,1)S(1)} %fusion) | data formatting | bytes 2359296 | tf_op jit(solution)/shard_map/convert_element_type | solution.py:733
  9.5 0.0 copy-done.2
  9.5 0.1 add.116
  9.7 0.1 broadcast_add_fusion
  9.8 0.7 add.120.wave_codes
  10.5 0.0 copy-start.1
  10.5 161.0 %shard_map.136 = bf16[32,144,128]{2,1,0:T(8,128)(2,1)} custom-call(bf16[32,144,128]{2,1,0:T(8,128)(2,1)} %bitcast.24, s32[4,1,640]{2,1,0:T(1,128)} %pad_add_fusion.codes, bf16[16,384]{1,0:T(8,128)(2,1)} %pad.24.area_part, bf16[384,512]{1,0:T(8,128)(2,1)} %constant.88.clone.pack_rows, bf16[384,384]{1,0:T(8,128)(2,1)} %constant.89.clone.unmix, ...), custom_call_target="tpu_custom_call" | custom-call | tf_op jit(solution)/shard_map/pallas_call | solution.py:588
  171.5 0.0 copy-done.1
  171.5 0.1 div.44
  171.6 2.0 %fusion.4 = bf16[32,72,64]{2,0,1:T(8,128)(2,1)S(1)} fusion(bf16[72,2,64,128]{3,2,1,0:T(8,128)(2,1)S(1)} %bitcast.23, bf16[32,72,2,128]{3,2,1,0:T(2,128)(2,1)} %bitcast.27, f32[72,64]{1,0:T(8,128)S(1)} %div.44), kind=kOutput, calls=%fused_computation.6 | convolution fusion | flops 75792384 | bytes 3852288 | tf_op jit(solution)/shard_map/fbkg,bkcg->fbc/dot_general | solution.py:749
  173.6 0.2 copy.23
  173.8 1.1 reshape.80
  (7 shorter events, 0.0 us)
Async XLA Ops:
  0.0 5.8 %copy-start = (bf16[144,64,128]{2,1,0:T(8,128)(2,1)S(1)}, bf16[144,64,128]{2,1,0:T(8,128)(2,1)}, u32[]{:S(2)}) copy-start(bf16[144,64,128]{2,1,0:T(8,128)(2,1)} %param.15) | copy-start | bytes 7077892
  7.6 1.9 %copy-start.2 = (s32[768]{0:T(1024)S(1)}, s32[768]{0:T(1024)}, u32[]{:S(2)}) copy-start(s32[768]{0:T(1024)} %wave_order.1) | copy-start | bytes 9220
  10.5 161.0 %copy-start.1 = (f32[4608]{0:T(1024)S(1)}, f32[4608]{0:T(1024)}, u32[]{:S(2)}) copy-start(f32[4608]{0:T(1024)} %param.18) | copy-start | bytes 55300

commit v3 on v2

--- a/solution.py
+++ b/solution.py
@@ -106,12 +106,13 @@
 def regrid(
     chunks,
     codes,
-    area_part,
+    band_area,
+    gauss_weight,
     pack_rows,
     unmix,
-    wave_codes,
+    wave_list,
     wave_order,
-    damping,
+    diffusion,
     legendre,
     order,
     back_order,
@@ -120,6 +121,7 @@
     code_in,
     code_rows,
     totals,
+    area_stage,
     area_in,
     area,
     table,
@@ -170,7 +172,16 @@
     per_row = lons // points
     greet()
 
-    area_in[chip] = area_part[...]
+    lat_dev, width = band_area.shape[0], lons // LEVS
+    row = lax.broadcasted_iota(jnp.int32, (PAD_LAT, half), 0)
+    own_lat = tile * lat_dev + row
+    north_lat = jnp.where(own_lat < half, own_lat, lats - 1 - own_lat)
+    found = lax.broadcasted_iota(jnp.int32, (PAD_LAT, half), 1) == north_lat
+    weight = jnp.sum(jnp.where(found, gauss_weight[...].reshape(1, half), 0.0), axis=1, keepdims=True)
+    area_stage[...] = jnp.ones_like(area_stage)
+    area_stage[:lat_dev] = band_area[:, pl.ds(pl.multiple_of(lev * width, width), width)]
+    real_row = lax.broadcasted_iota(jnp.int32, (PAD_LAT, width), 0) < lat_dev
+    area_in[chip] = jnp.where(real_row, weight / area_stage[...], 0.0).astype(BF)
 
     def area_z(step):
         there = chip_at(x, z + step)
@@ -204,25 +215,29 @@
     keep_tables = pltpu.make_async_copy(legendre, own_tables(0, own), local_sem.at[0])
     keep_tables.start()
 
+    unit = own // 6
+    give_order = (((0, 2), (2, 4)), ((3, 2), (5, 1), (0, 3)))
+
     def give_tables(piece, way):
-        first, count = ((0, own // 6), (own // 6, own - own // 6))[piece]
+        first, count = (unit * v for v in give_order[way][piece])
         return remote(
             legendre.at[pl.ds(first, count)],
             own_tables(first, count),
             table_send.at[0],
-            table_recv.at[way],
+            table_recv.at[2 * way + min(piece, 1)],
             tile,
             (lev + (1, LEVS - 1)[way]) % LEVS,
         )
 
-    def pass_tables(way):
+    def pass_tables(piece, way):
         from_lev = (lev + (LEVS - 1, 1)[way]) % LEVS
-        here = tables.at[pl.ds(own * from_lev + way * (own // 2), own // 2)]
+        first, count = ((0, 2), (2, 1))[piece]
+        here = tables.at[pl.ds(own * from_lev + (3 * way + first) * unit, count * unit)]
         return remote(
             here,
             here,
             table_send.at[0],
-            table_recv.at[2],
+            table_recv.at[4],
             tile,
             (lev + (1, LEVS - 1)[way]) % LEVS,
         )
@@ -267,6 +282,12 @@
     arrived[0] = chunks[chip]
 
     slots = response.shape[0]
+
+    found = lax.broadcasted_iota(jnp.int32, (CHIPS, LEVS * CHIPS), 1) == (
+        lax.broadcasted_iota(jnp.int32, (CHIPS, LEVS * CHIPS), 0) + CHIPS * lev
+    )
+    damping = diffusion[...].reshape(1, LEVS * CHIPS)
+    damping = jnp.sum(jnp.where(found, damping, 0.0), axis=1, keepdims=True)
 
     def make_response(slot, carry):
         wave = wave_order[tile * slots + slot]
@@ -274,7 +295,7 @@
         for p in range(2):
             degree = wave + p + 2 * lax.broadcasted_iota(jnp.int32, (1, half), 1)
             growth = (degree * (degree + 1)).astype(F32) * (1.0 / (TRUNC * (TRUNC + 1)))
-            value = doubled / (1.0 + damping[...] * growth)
+            value = doubled / (1.0 + damping * growth)
             response[slot, p] = jnp.where(degree <= TRUNC, value, 0.0)
         return carry
 
@@ -287,13 +308,16 @@
     strip = points
     longitude = lax.broadcasted_iota(jnp.int32, (strip, points), 1)
     norm = 1.0 / math.sqrt(lons)
+    waves = wave_list[...].reshape(1, TILES * slots).astype(F32)
+    wave_at = lax.broadcasted_iota(jnp.int32, (strip, TILES * slots), 1)
 
     def make_rows(step, carry):
         at = pl.ds(pl.multiple_of(step * strip, strip), strip)
-        code = wave_codes[:, at]
-        code = down_rows(code // 64, points) * 64.0 + down_rows(code % 64, points)
-        code = code.astype(jnp.int32)
-        wave, part = code % 1024, code // 1024
+        row = step * strip + lax.broadcasted_iota(jnp.int32, (strip, 1), 0)
+        part = row // slots % 2
+        found = wave_at == row // (2 * slots) * slots + row % slots
+        wave = jnp.sum(jnp.where(found, waves, 0.0), axis=1, keepdims=True).astype(jnp.int32)
+        wave = jnp.broadcast_to(wave, (strip, points))
         cos, sin = cos_sin(wrap(wave * longitude + part * (lons // 4), lons), lons)
         cos, sin = cos * norm, sin * norm
         turn_c, turn_s = cos_sin(wrap(wave * points, lons), lons)
@@ -311,8 +335,8 @@
     area_core(lev).start()
     for step in range(1, LEVS):
         area_y(step).start()
-    for way in range(2):
-        give_tables(1, way).start()
+    for piece, way in ((1, 0), (1, 1), (2, 1)):
+        give_tables(piece, way).start()
 
     lat_index = lax.broadcasted_iota(jnp.int32, (lats, rows), 0)
 
@@ -354,6 +378,9 @@
     add_group(0, True)
     lax.fori_loop(1, 4, later_group, 0)
     drain(area.at[pl.ds(0, LEVS - 1), core], area_recv.at[2])
+    for way in range(2):
+        drain(tables.at[pl.ds(0, 2 * unit)], table_recv.at[2 * way])
+        pass_tables(0, way).start()
     for step in range(1, LEVS):
         area_core((lev + step) % LEVS).start()
     lax.fori_loop(4, CHIPS // GROUP, later_group, 0)
@@ -361,7 +388,6 @@
 
     sign = (1 - 2 * core).astype(F32)
     quarters = LEVS
-    width = lons // LEVS
 
     def weights(q, side):
         at = slice(side * (half // 2), (side + 1) * (half // 2))
@@ -421,8 +447,8 @@
     lax.fori_loop(0, XS, transform, 0)
     spectra[slot_of(tile)] = fourier[tile]
     for way in range(2):
-        drain(tables.at[pl.ds(0, own)], table_recv.at[way])
-        pass_tables(way).start()
+        drain(tables.at[pl.ds(0, 4 * unit)], table_recv.at[2 * way + 1])
+        pass_tables(1, way).start()
 
     drain(spectra.at[pl.ds(0, TILES - 1)], fourier_recv.at[0])
 
@@ -432,13 +458,16 @@
         )
 
     mixed = 2 * CHIPS
-    drain(tables.at[pl.ds(0, own)], table_recv.at[2])
     keep_tables.wait()
+    own_slots = slots // LEVS
     for p in range(2):
         rows_in = spectra[p * CHIPS : (p + 1) * CHIPS].reshape(CHIPS * share, half)
         sorted_in[...] = jnp.dot(order[...], rows_in, preferred_element_type=F32).astype(BF)
 
-        def one_slot(slot, carry):
+        def one_slot(step, carry):
+            there = step // own_slots
+            there = (lev + there + there // 2 * (5 - 2 * there)) % LEVS
+            slot = there * own_slots + step % own_slots
             at = pl.ds(pl.multiple_of(slot * mixed, mixed), mixed)
             legendre_at = tables[2 * slot + p]
             coefficient = lax.dot_general(
@@ -453,7 +482,10 @@
             ).astype(BF)
             return carry
 
-        lax.fori_loop(0, slots, one_slot, 0)
+        lax.fori_loop(0, slots - own_slots, one_slot, 0)
+        if p == 0:
+            drain(tables.at[pl.ds(0, own)], table_recv.at[4])
+        lax.fori_loop(slots - own_slots, slots, one_slot, 0)
 
         def send_back(step, carry):
             first = ((x + step) % XS) * ZS
@@ -573,12 +605,12 @@
     drain(tables.at[pl.ds(0, 3 * own)], table_send.at[0])
 
 
-def regrid_call(chunks, codes, area_part, lat_dev, wave_codes, wave_order, damping, legendre):
+def regrid_call(chunks, codes, band_area, gauss_weight, wave_order, diffusion, legendre):
     pairs, points = chunks.shape[1:]
-    room, width = codes.shape[2], area_part.shape[1]
-    lons, lats = LEVS * width, lat_dev * TILES
-    half, share, groups = lats // 2, wave_codes.shape[1] // TILES, CHIPS // GROUP
-    slots, mixed = share // 2, CHIPS * share
+    room, (lat_dev, lons) = codes.shape[2], band_area.shape
+    width, lats = lons // LEVS, lat_dev * TILES
+    half, slots, groups = lats // 2, wave_order.shape[0] // TILES, CHIPS // GROUP
+    share, mixed = 2 * slots, CHIPS * 2 * slots
     order, back_order = slot_orders(slots)
     pack_rows, unmix = lat_orders(lat_dev)
     vmem = pl.BlockSpec(memory_space=pltpu.VMEM)
@@ -588,13 +620,14 @@
     return pl.pallas_call(
         regrid,
         out_shape=jax.ShapeDtypeStruct((CHIPS, pairs, points), BF),
-        in_specs=[vmem] * 6 + [smem, vmem, anywhere, vmem, vmem],
+        in_specs=[vmem] * 7 + [smem, vmem, anywhere, vmem, vmem],
         out_specs=vmem,
         scratch_shapes=[
             pltpu.VMEM((CHIPS, pairs, points), BF),
             pltpu.VMEM((CHIPS, 1, room), jnp.int32),
             pltpu.VMEM((groups, 1, room), jnp.int32),
             pltpu.VMEM((lats, lons), F32),
+            pltpu.VMEM((PAD_LAT, width), F32),
             pltpu.VMEM((CHIPS, PAD_LAT, width), BF),
             pltpu.VMEM((LEVS, 2, half, width), BF),
             pltpu.VMEM((TILES * share, lons), BF),
@@ -621,7 +654,7 @@
             dma((4,)),
             dma((4,)),
             dma((1,)),
-            dma((3,)),
+            dma((5,)),
             dma((1,)),
             dma((LEVS,)),
             dma((1,)),
@@ -640,12 +673,13 @@
     )(
         chunks,
         codes,
-        area_part,
+        band_area,
+        gauss_weight,
         pack_rows,
         unmix,
-        wave_codes,
         wave_order,
-        damping,
+        wave_order,
+        diffusion,
         legendre,
         order,
         back_order,
@@ -695,9 +729,6 @@
     gauss_weight,
     diffusion,
 ):
-    levs = lax.axis_size("lev")
-    tile, x, z, core = place()
-    lev = lax.axis_index("lev")
     fields, cell_count = cube_field.shape
     pairs, cells, points = margin.shape
     blocks = pairs // 2
@@ -705,8 +736,6 @@
     per_row = lons // points
     lats = lat_dev * TILES
     half = lats // 2
-    slots = wave_order.shape[0] // TILES
-    width = lons // levs
 
     lat = pair_owner * lat_dev + pair_block // per_row
     south = jnp.where(lat < half, 0, half)
@@ -718,11 +747,6 @@
         [jnp.pad(code, (j * pairs, room - (j + 1) * pairs))[None] for j in range(GROUP)]
     )
 
-    own_lat = tile * lat_dev + jnp.arange(lat_dev, dtype=jnp.int32)
-    own_weight = gauss_weight[jnp.where(own_lat < half, own_lat, lats - 1 - own_lat)]
-    part = lax.dynamic_slice_in_dim(band_area, lev * width, width, axis=1)
-    part = (own_weight[:, None] / part).astype(BF)
-    area_part = jnp.pad(part, ((0, PAD_LAT - lat_dev), (0, 0)))
     margin_q = margin.reshape(blocks, 2, cells, points)
     chunks = jnp.einsum(
         "fbc,bkcg->fbkg",
@@ -732,17 +756,13 @@
     )
     chunks = chunks.astype(BF).reshape(fields, pairs, points)
 
-    part_codes = jnp.arange(2, dtype=jnp.int32)[None, :, None] * 1024
-    wave_codes = (wave_order.reshape(TILES, 1, slots) + part_codes).reshape(1, -1)
-    damping = lax.dynamic_slice_in_dim(diffusion, lev * fields, fields)[:, None]
     replies = regrid_call(
         chunks,
         codes,
-        area_part,
-        lat_dev,
-        wave_codes,
+        band_area,
+        gauss_weight,
         wave_order,
-        damping,
+        diffusion,
         legendre.reshape(-1, half, half),
     )
 

time: 177 us -> 165 us (0.932)
  Pallas kernels: 161 us -> 155 us
  local copies, waits for them, and re-layouts: 9.09 us -> 4.84 us
    pallas_call x1, Pallas kernels: 161 us -> 155 us  [regrid_call(): pl.pallas_call(regrid, out_shape=jax.ShapeDtypeStruct((CHIPS, pairs, poin...]
where the time goes in v3:
time: 165 us; the launch traced here: 164 us
  Pallas kernels  155 us (94%)
  local copies, waits for them, and re-layouts  4.84 us (3%)
  matrix products  2.47 us (1%)
    pallas_call x1, Pallas kernels, regrid_call(): pl.pallas_call(regrid, out_shape=jax.ShapeDtypeStruct((CHIPS, pairs, poin...  155 us

profile of v3, /device:TPU:1, one launch (start us, length us, event | category | flops | bytes accessed | tf_op | source)
XLA Modules:
  0.0 163.7 jit_solution(18278630999175607083)
XLA Ops:
  0.0 0.0 copy-start
  0.0 0.9 fusion.11
  0.9 0.1 fusion.12
  1.0 0.6 pad_add_fusion.codes
  1.6 0.1 copy-done
  1.7 1.3 reshape.20
  3.0 0.5 fusion
  3.5 1.9 %copy.19 = bf16[32,72,2,128]{3,2,1,0:T(2,128)(2,1)} copy(bf16[32,72,2,128]{3,0,2,1:T(8,128)(2,1)S(1)} %fusion) | data formatting | bytes 2359296 | tf_op jit(solution)/shard_map/convert_element_type | solution.py:757
  5.4 0.0 copy-start.1
  5.4 154.8 %shard_map.136 = bf16[32,144,128]{2,1,0:T(8,128)(2,1)} custom-call(bf16[32,144,128]{2,1,0:T(8,128)(2,1)} %bitcast.20, s32[4,1,640]{2,1,0:T(1,128)} %pad_add_fusion.codes, f32[12,1536]{1,0:T(8,128)} %band_area.1, f32[384]{0:T(512)} %gauss_weight.1, bf16[384,512]{1,0:T(8,128)(2,1)} %constant.67.clone.pack_rows, bf16[384,384]{1,0:T(8,128)(2,1)} %constant.68.clone.unmix, ...), custom_call_target="tpu_custom_call" | custom-call | tf_op jit(solution)/shard_map/pallas_call | solution.py:620
  160.3 0.0 copy-done.1
  160.3 0.1 div.34
  160.4 2.0 %fusion.4 = bf16[32,72,64]{2,0,1:T(8,128)(2,1)S(1)} fusion(bf16[72,2,64,128]{3,2,1,0:T(8,128)(2,1)S(1)} %bitcast.19, bf16[32,72,2,128]{3,2,1,0:T(2,128)(2,1)} %bitcast.23, f32[72,64]{1,0:T(8,128)S(1)} %div.34), kind=kOutput, calls=%fused_computation.5 | convolution fusion | flops 75792384 | bytes 3852288 | tf_op jit(solution)/shard_map/fbkg,bkcg->fbc/dot_general | solution.py:769
  162.4 0.2 copy.21
  162.6 1.1 reshape.24
  (4 shorter events, 0.0 us)
Async XLA Ops:
  0.0 1.7 %copy-start = (bf16[144,64,128]{2,1,0:T(8,128)(2,1)S(1)}, bf16[144,64,128]{2,1,0:T(8,128)(2,1)}, u32[]{:S(2)}) copy-start(bf16[144,64,128]{2,1,0:T(8,128)(2,1)} %param.15) | copy-start | bytes 7077892
  5.4 154.9 %copy-start.1 = (f32[4608]{0:T(1024)S(1)}, f32[4608]{0:T(1024)}, u32[]{:S(2)}) copy-start(f32[4608]{0:T(1024)} %param.18) | copy-start | bytes 55300

commit v4 on v3

--- a/solution.py
+++ b/solution.py
@@ -48,7 +48,10 @@
     for step in range(1, LEVS):
         peer = (tile, (lev + step) % LEVS)
         pl.semaphore_signal(barrier, inc=1, device_id=peer, device_id_type=MESH)
-    pl.semaphore_wait(barrier, TILES - 1 + LEVS - 1)
+
+
+def welcome():
+    pl.semaphore_wait(pltpu.get_barrier_semaphore(), TILES - 1 + LEVS - 1)
 
 
 def remote(src, dst, send, recv, peer, lev=None):
@@ -104,8 +107,10 @@
 
 
 def regrid(
-    chunks,
-    codes,
+    cube_field,
+    margin,
+    pair_owner,
+    pair_block,
     band_area,
     gauss_weight,
     pack_rows,
@@ -114,9 +119,13 @@
     wave_order,
     diffusion,
     legendre,
+    order_any,
+    back_order_any,
+    replies,
+    chunks,
+    codes,
     order,
     back_order,
-    replies,
     arrived,
     code_in,
     code_rows,
@@ -171,8 +180,45 @@
     rows = GROUP * pairs
     per_row = lons // points
     greet()
+    orders = [
+        pltpu.make_async_copy(order_any, order, local_sem.at[1]),
+        pltpu.make_async_copy(back_order_any, back_order, local_sem.at[2]),
+    ]
+    for copy in orders:
+        copy.start()
 
     lat_dev, width = band_area.shape[0], lons // LEVS
+    owner, block = pair_owner[...].reshape(1, pairs), pair_block[...].reshape(1, pairs)
+    lat = owner * lat_dev + block // per_row
+    south_side = jnp.where(lat < half, 0, half)
+    north_lat = jnp.where(lat < half, lat, lats - 1 - lat)
+    code = (south_side + mixed_row(north_lat, lat_dev)) * 1024 + south_side + north_lat
+    codes[...] = jnp.zeros_like(codes)
+    codes[0, :, :pairs] = code * 16 + block % per_row
+    code = jnp.broadcast_to(codes[0], (8, codes.shape[2]))
+    for j in range(1, GROUP):
+        codes[j] = pltpu.roll(code, j * pairs, 1)[:1]
+
+    cells = margin.shape[2]
+    span = 8 * cells
+    pair_at = lax.broadcasted_iota(jnp.int32, (16, span), 0)
+    block_at = lax.broadcasted_iota(jnp.int32, (16, span), 1) // cells
+    masks = [jnp.where(2 * block_at + k == pair_at, 1.0, 0.0).astype(F32) for k in range(2)]
+
+    def contribute(step, carry):
+        field = cube_field[:, pl.ds(pl.multiple_of(step * span, span), span)].astype(F32)
+        total = None
+        for k in range(2):
+            spread = (field[:, None, :] * masks[k][None]).reshape(CHIPS * 16, span).astype(BF)
+            weights_k = margin[pl.ds(step * 8, 8), k].reshape(span, points)
+            term = jnp.dot(spread, weights_k, preferred_element_type=F32)
+            total = term if total is None else total + term
+        at = pl.ds(pl.multiple_of(step * 16, 16), 16)
+        chunks[:, at, :] = total.astype(BF).reshape(CHIPS, 16, points)
+        return carry
+
+    lax.fori_loop(0, pairs // 16, contribute, 0)
+
     row = lax.broadcasted_iota(jnp.int32, (PAD_LAT, half), 0)
     own_lat = tile * lat_dev + row
     north_lat = jnp.where(own_lat < half, own_lat, lats - 1 - own_lat)
@@ -182,6 +228,8 @@
     area_stage[:lat_dev] = band_area[:, pl.ds(pl.multiple_of(lev * width, width), width)]
     real_row = lax.broadcasted_iota(jnp.int32, (PAD_LAT, width), 0) < lat_dev
     area_in[chip] = jnp.where(real_row, weight / area_stage[...], 0.0).astype(BF)
+
+    welcome()
 
     def area_z(step):
         there = chip_at(x, z + step)
@@ -459,6 +507,8 @@
 
     mixed = 2 * CHIPS
     keep_tables.wait()
+    for copy in orders:
+        copy.wait()
     own_slots = slots // LEVS
     for p in range(2):
         rows_in = spectra[p * CHIPS : (p + 1) * CHIPS].reshape(CHIPS * share, half)
@@ -605,9 +655,20 @@
     drain(tables.at[pl.ds(0, 3 * own)], table_send.at[0])
 
 
-def regrid_call(chunks, codes, band_area, gauss_weight, wave_order, diffusion, legendre):
-    pairs, points = chunks.shape[1:]
-    room, (lat_dev, lons) = codes.shape[2], band_area.shape
+def regrid_call(
+    cube_field,
+    margin,
+    pair_owner,
+    pair_block,
+    band_area,
+    gauss_weight,
+    wave_order,
+    diffusion,
+    legendre,
+):
+    pairs, points = pair_owner.shape[0], margin.shape[3]
+    lat_dev, lons = band_area.shape
+    room = -(-GROUP * pairs // points) * points
     width, lats = lons // LEVS, lat_dev * TILES
     half, slots, groups = lats // 2, wave_order.shape[0] // TILES, CHIPS // GROUP
     share, mixed = 2 * slots, CHIPS * 2 * slots
@@ -620,9 +681,13 @@
     return pl.pallas_call(
         regrid,
         out_shape=jax.ShapeDtypeStruct((CHIPS, pairs, points), BF),
-        in_specs=[vmem] * 7 + [smem, vmem, anywhere, vmem, vmem],
+        in_specs=[vmem] * 9 + [smem, vmem, anywhere, anywhere, anywhere],
         out_specs=vmem,
         scratch_shapes=[
+            pltpu.VMEM((CHIPS, pairs, points), BF),
+            pltpu.VMEM((GROUP, 1, room), jnp.int32),
+            pltpu.VMEM((mixed, mixed), BF),
+            pltpu.VMEM((mixed, mixed), BF),
             pltpu.VMEM((CHIPS, pairs, points), BF),
             pltpu.VMEM((CHIPS, 1, room), jnp.int32),
             pltpu.VMEM((groups, 1, room), jnp.int32),
@@ -665,14 +730,16 @@
             dma((LEVS,)),
             dma((1,)),
             dma((1,)),
-            dma((1,)),
+            dma((3,)),
         ],
         compiler_params=pltpu.CompilerParams(
             collective_id=0, has_side_effects=True, vmem_limit_bytes=VMEM_LIMIT
         ),
     )(
-        chunks,
-        codes,
+        cube_field,
+        margin,
+        pair_owner,
+        pair_block,
         band_area,
         gauss_weight,
         pack_rows,
@@ -737,28 +804,12 @@
     lats = lat_dev * TILES
     half = lats // 2
 
-    lat = pair_owner * lat_dev + pair_block // per_row
-    south = jnp.where(lat < half, 0, half)
-    north = jnp.where(lat < half, lat, lats - 1 - lat)
-    code = (south + mixed_row(north, lat_dev)) * 1024 + south + north
-    code = code * 16 + pair_block % per_row
-    room = -(-GROUP * pairs // points) * points
-    codes = jnp.stack(
-        [jnp.pad(code, (j * pairs, room - (j + 1) * pairs))[None] for j in range(GROUP)]
-    )
-
     margin_q = margin.reshape(blocks, 2, cells, points)
-    chunks = jnp.einsum(
-        "fbc,bkcg->fbkg",
-        cube_field.reshape(fields, blocks, cells),
+    replies = regrid_call(
+        cube_field,
         margin_q,
-        preferred_element_type=F32,
-    )
-    chunks = chunks.astype(BF).reshape(fields, pairs, points)
-
-    replies = regrid_call(
-        chunks,
-        codes,
+        pair_owner,
+        pair_block,
         band_area,
         gauss_weight,
         wave_order,

time: 165 us -> 162 us (0.982)
  local copies, waits for them, and re-layouts: 4.84 us -> 2.12 us
  Pallas kernels: 155 us -> 157 us
    convert_element_type x1 -> x0, local copies, waits for them, and re-layouts: 1.93 us -> none  [shards(): chunks = chunks.astype(BF).reshape(fields, pairs, points)]
    pallas_call x1, Pallas kernels: 155 us -> 157 us  [regrid_call(): pl.pallas_call(regrid, out_shape=jax.ShapeDtypeStruct((CHIPS, pairs, poin...]
where the time goes in v4:
time: 162 us; the launch traced here: 161 us
  Pallas kernels  157 us (97%)
  local copies, waits for them, and re-layouts  2.12 us (1%)
  matrix products  2.02 us (1%)
    pallas_call x1, Pallas kernels, regrid_call(): pl.pallas_call(regrid, out_shape=jax.ShapeDtypeStruct((CHIPS, pairs, poin...  157 us

profile of v4, /device:TPU:1, one launch (start us, length us, event | category | flops | bytes accessed | tf_op | source)
XLA Modules:
  0.0 160.7 jit_solution(11089589917315996)
XLA Ops:
  0.0 0.8 div.11
  0.8 0.0 copy-start
  0.8 156.5 %shard_map.136 = bf16[32,144,128]{2,1,0:T(8,128)(2,1)} custom-call(bf16[32,4608]{1,0:T(8,128)(2,1)} %cube_field.1, bf16[72,2,64,128]{3,2,1,0:T(8,128)(2,1)} %bitcast.13, s32[144]{0:T(256)} %pair_owner.1, s32[144]{0:T(256)} %pair_block.1, f32[12,1536]{1,0:T(8,128)} %band_area.1, f32[384]{0:T(512)} %gauss_weight.1, bf16[384,512]{1,0:T(8,128)(2,1)} %constant.10.clone.pack_rows, ...), custom_call_target="tpu_custom_call" | custom-call | tf_op jit(solution)/shard_map/pallas_call | solution.py:681
  157.3 0.0 copy-done
  157.3 2.0 %fusion.3 = bf16[32,72,64]{2,0,1:T(8,128)(2,1)S(1)} fusion(bf16[72,2,64,128]{3,2,1,0:T(8,128)(2,1)S(1)} %bitcast.14, bf16[32,72,2,128]{3,2,1,0:T(2,128)(2,1)} %bitcast.16, f32[72,64]{1,0:T(8,128)S(1)} %div.11), kind=kOutput, calls=%fused_computation.3 | convolution fusion | flops 75792384 | bytes 3852288 | tf_op jit(solution)/shard_map/fbkg,bkcg->fbc/dot_general | solution.py:820
  159.3 0.2 copy.17
  159.6 1.1 reshape.16
Async XLA Ops:
  0.8 156.5 %copy-start = (bf16[144,64,128]{2,1,0:T(8,128)(2,1)S(1)}, bf16[144,64,128]{2,1,0:T(8,128)(2,1)}, u32[]{:S(2)}) copy-start(bf16[144,64,128]{2,1,0:T(8,128)(2,1)} %param.15) | copy-start | bytes 7077892

commit v5 on v4

--- a/solution.py
+++ b/solution.py
@@ -107,8 +107,8 @@
 
 
 def regrid(
-    cube_field,
-    margin,
+    cube_any,
+    margin_any,
     pair_owner,
     pair_block,
     band_area,
@@ -122,6 +122,8 @@
     order_any,
     back_order_any,
     replies,
+    cube_field,
+    margin,
     chunks,
     codes,
     order,
@@ -179,6 +181,12 @@
     pairs, points = arrived.shape[1:]
     rows = GROUP * pairs
     per_row = lons // points
+    fields_in = [
+        pltpu.make_async_copy(cube_any, cube_field, local_sem.at[3]),
+        pltpu.make_async_copy(margin_any, margin, local_sem.at[4]),
+    ]
+    for copy in fields_in:
+        copy.start()
     greet()
     orders = [
         pltpu.make_async_copy(order_any, order, local_sem.at[1]),
@@ -217,6 +225,8 @@
         chunks[:, at, :] = total.astype(BF).reshape(CHIPS, 16, points)
         return carry
 
+    for copy in fields_in:
+        copy.wait()
     lax.fori_loop(0, pairs // 16, contribute, 0)
 
     row = lax.broadcasted_iota(jnp.int32, (PAD_LAT, half), 0)
@@ -532,10 +542,10 @@
             ).astype(BF)
             return carry
 
-        lax.fori_loop(0, slots - own_slots, one_slot, 0)
+        lax.fori_loop(0, slots - own_slots, one_slot, 0, unroll=own_slots)
         if p == 0:
             drain(tables.at[pl.ds(0, own)], table_recv.at[4])
-        lax.fori_loop(slots - own_slots, slots, one_slot, 0)
+        lax.fori_loop(slots - own_slots, slots, one_slot, 0, unroll=own_slots)
 
         def send_back(step, carry):
             first = ((x + step) % XS) * ZS
@@ -681,9 +691,11 @@
     return pl.pallas_call(
         regrid,
         out_shape=jax.ShapeDtypeStruct((CHIPS, pairs, points), BF),
-        in_specs=[vmem] * 9 + [smem, vmem, anywhere, anywhere, anywhere],
+        in_specs=[anywhere] * 2 + [vmem] * 7 + [smem, vmem, anywhere, anywhere, anywhere],
         out_specs=vmem,
         scratch_shapes=[
+            pltpu.VMEM(cube_field.shape, BF),
+            pltpu.VMEM(margin.shape, BF),
             pltpu.VMEM((CHIPS, pairs, points), BF),
             pltpu.VMEM((GROUP, 1, room), jnp.int32),
             pltpu.VMEM((mixed, mixed), BF),
@@ -730,7 +742,7 @@
             dma((LEVS,)),
             dma((1,)),
             dma((1,)),
-            dma((3,)),
+            dma((5,)),
         ],
         compiler_params=pltpu.CompilerParams(
             collective_id=0, has_side_effects=True, vmem_limit_bytes=VMEM_LIMIT

time: 162 us -> 160 us (0.988)
  Pallas kernels: 157 us -> 154 us
    pallas_call x1, Pallas kernels: 157 us -> 154 us  [regrid_call(): pl.pallas_call(regrid, out_shape=jax.ShapeDtypeStruct((CHIPS, pairs, poin...]
where the time goes in v5:
time: 160 us; the launch traced here: 158 us
  Pallas kernels  154 us (96%)
  local copies, waits for them, and re-layouts  2.12 us (1%)
  matrix products  2.01 us (1%)
    pallas_call x1, Pallas kernels, regrid_call(): pl.pallas_call(regrid, out_shape=jax.ShapeDtypeStruct((CHIPS, pairs, poin...  154 us

profile of v5, /device:TPU:1, one launch (start us, length us, event | category | flops | bytes accessed | tf_op | source)
XLA Modules:
  0.0 158.5 jit_solution(8616248901365786856)
XLA Ops:
  0.0 0.8 div.11
  0.8 0.0 copy-start
  0.8 154.3 %shard_map.136 = bf16[32,144,128]{2,1,0:T(8,128)(2,1)} custom-call(bf16[32,4608]{1,0:T(8,128)(2,1)} %cube_any.1, bf16[72,2,64,128]{3,2,1,0:T(8,128)(2,1)} %bitcast.13, s32[144]{0:T(256)} %pair_owner.1, s32[144]{0:T(256)} %pair_block.1, f32[12,1536]{1,0:T(8,128)} %band_area.1, f32[384]{0:T(512)} %gauss_weight.1, bf16[384,512]{1,0:T(8,128)(2,1)} %constant.10.clone.pack_rows, ...), custom_call_target="tpu_custom_call" | custom-call | tf_op jit(solution)/shard_map/pallas_call | solution.py:691
  155.1 0.0 copy-done
  155.2 2.0 %fusion.3 = bf16[32,72,64]{2,0,1:T(8,128)(2,1)S(1)} fusion(bf16[72,2,64,128]{3,2,1,0:T(8,128)(2,1)S(1)} %bitcast.14, bf16[32,72,2,128]{3,2,1,0:T(2,128)(2,1)} %bitcast.16, f32[72,64]{1,0:T(8,128)S(1)} %div.11), kind=kOutput, calls=%fused_computation.3 | convolution fusion | flops 75792384 | bytes 3852288 | tf_op jit(solution)/shard_map/fbkg,bkcg->fbc/dot_general | solution.py:832
  157.2 0.2 copy.17
  157.4 1.1 reshape.16
Async XLA Ops:
  0.8 154.3 %copy-start = (bf16[144,64,128]{2,1,0:T(8,128)(2,1)S(1)}, bf16[144,64,128]{2,1,0:T(8,128)(2,1)}, u32[]{:S(2)}) copy-start(bf16[144,64,128]{2,1,0:T(8,128)(2,1)} %param.15) | copy-start | bytes 7077892

commit v6 on v5

--- a/solution.py
+++ b/solution.py
@@ -227,7 +227,7 @@
 
     for copy in fields_in:
         copy.wait()
-    lax.fori_loop(0, pairs // 16, contribute, 0)
+    lax.fori_loop(0, pairs // 16, contribute, 0, unroll=3)
 
     row = lax.broadcasted_iota(jnp.int32, (PAD_LAT, half), 0)
     own_lat = tile * lat_dev + row
@@ -357,7 +357,7 @@
             response[slot, p] = jnp.where(degree <= TRUNC, value, 0.0)
         return carry
 
-    lax.fori_loop(0, slots, make_response, 0)
+    lax.fori_loop(0, slots, make_response, 0, unroll=3)
 
     drain(area_in.at[pl.ds(0, ZS - 1)], area_recv.at[0])
     for step in range(1, XS):
@@ -384,7 +384,7 @@
             cos, sin = cos * turn_c - sin * turn_s, sin * turn_c + cos * turn_s
         return carry
 
-    lax.fori_loop(0, table.shape[0] // strip, make_rows, 0)
+    lax.fori_loop(0, table.shape[0] // strip, make_rows, 0, unroll=3)
 
     drain(area_in.at[pl.ds(0, CHIPS - ZS)], area_recv.at[1])
     area[lev, core] = jnp.dot(

time: 160 us -> 158 us (0.988)
  no operation moved by 1% of the time
where the time goes in v6:
time: 158 us
  Pallas kernels  154 us (97%)
  local copies, waits for them, and re-layouts  2.12 us (1%)
  matrix products  2.02 us (1%)
    pallas_call x1, Pallas kernels, regrid_call(): pl.pallas_call(regrid, out_shape=jax.ShapeDtypeStruct((CHIPS, pairs, poin...  154 us

profile of v6, /device:TPU:1, one launch (start us, length us, event | category | flops | bytes accessed | tf_op | source)
XLA Modules:
  0.0 157.9 jit_solution(1430702628361440043)
XLA Ops:
  0.0 0.8 div.11
  0.8 0.0 copy-start
  0.8 153.8 %shard_map.136 = bf16[32,144,128]{2,1,0:T(8,128)(2,1)} custom-call(bf16[32,4608]{1,0:T(8,128)(2,1)} %cube_any.1, bf16[72,2,64,128]{3,2,1,0:T(8,128)(2,1)} %bitcast.13, s32[144]{0:T(256)} %pair_owner.1, s32[144]{0:T(256)} %pair_block.1, f32[12,1536]{1,0:T(8,128)} %band_area.1, f32[384]{0:T(512)} %gauss_weight.1, bf16[384,512]{1,0:T(8,128)(2,1)} %constant.10.clone.pack_rows, ...), custom_call_target="tpu_custom_call" | custom-call | tf_op jit(solution)/shard_map/pallas_call | solution.py:691
  154.6 0.0 copy-done
  154.6 2.0 %fusion.3 = bf16[32,72,64]{2,0,1:T(8,128)(2,1)S(1)} fusion(bf16[72,2,64,128]{3,2,1,0:T(8,128)(2,1)S(1)} %bitcast.14, bf16[32,72,2,128]{3,2,1,0:T(2,128)(2,1)} %bitcast.16, f32[72,64]{1,0:T(8,128)S(1)} %div.11), kind=kOutput, calls=%fused_computation.3 | convolution fusion | flops 75792384 | bytes 3852288 | tf_op jit(solution)/shard_map/fbkg,bkcg->fbc/dot_general | solution.py:832
  156.6 0.2 copy.17
  156.9 1.1 reshape.16
Async XLA Ops:
  0.8 153.8 %copy-start = (bf16[144,64,128]{2,1,0:T(8,128)(2,1)S(1)}, bf16[144,64,128]{2,1,0:T(8,128)(2,1)}, u32[]{:S(2)}) copy-start(bf16[144,64,128]{2,1,0:T(8,128)(2,1)} %param.15) | copy-start | bytes 7077892
